TPU v7x, 128 devices: a whole 4x4x4 slice. The times are simulated.
128 devices in a mesh: af: 16 (over y_hi, x, core), gz: 8 (over z, y_lo).
Axes of the slice: x: 4, y: 4 (y_hi: 2, y_lo: 2; y = y_hi * 2 + y_lo), z: 4, core: 2. Of those that a mesh axis runs over, the one named last changes fastest.
Arguments:
- inputs: bfloat16 [512, 32, 1024], P('af', 'gz'), may hold values from -6 to 6
- preact: bfloat16 [512, 32, 1024], P('af', 'gz'), may hold values from -6 to 6
- cotangent: bfloat16 [512, 32, 1024], P('af', 'gz'), may hold values from -6 to 6
- weight1: bfloat16 [3, 3, 3, 512, 512], P(None, None, None, 'af'), may hold values from -0.0546875 to 0.0546875
- weight2: bfloat16 [3, 3, 3, 512, 512], P(None, None, None, 'af'), may hold values from -0.0546875 to 0.0546875
Outputs:
- input_grad: bfloat16 [32, 32, 32, 512], P('gz', 'af')
- filter1_grad: float32 [3, 3, 3, 512, 512], P(None, None, None, ('af', 'gz'))
- filter2_grad: float32 [3, 3, 3, 512, 512], P(None, None, None, ('af', 'gz'))
All inputs are finite; a program needn't handle non-finite values.
Results may differ from a plain program's by a relative error of at most 0.017.
Values may be sent and summed in bfloat16 or wider, within the bound.
No kernel may reach another device: no remote copies, remote signals or barrier semaphores. Data moves between devices by JAX's collectives and lax.ppermute only.
A program may use at most 256 MiB of HBM per device.

v0:
```python
import functools

import jax
import jax.numpy as jnp
from jax import lax
from jax.experimental import pallas as pl
from jax.experimental.pallas import tpu as pltpu
from jax.sharding import Mesh
from jax.sharding import PartitionSpec as P

AF = ("yh", "x", "core")
GZ = ("z", "yl")
SIZE = {"yh": 2, "x": 4, "core": 2, "z": 4, "yl": 2}
ROW = 32
CELLS = 1024
TAPS = 9
BLOCK = 32
WIDE = 128
DEPTH = 4
SRC = 4
DEEP = TAPS * BLOCK
K = SRC * DEEP
VMEM_BYTES = 48 * 1024 * 1024
NN = (((1,), (0,)), ((), ()))
NT = (((1,), (1,)), ((), ()))
F32 = jnp.float32
BF16 = jnp.bfloat16


def params():
    return pltpu.CompilerParams(vmem_limit_bytes=VMEM_BYTES)


def whole(count):
    return [pl.BlockSpec(memory_space=pltpu.VMEM)] * count


def from_ahead(value, axis, step):
    n = SIZE[axis]
    return lax.ppermute(value, axis, [(i, (i - step) % n) for i in range(n)])


def shape(dims, kind=BF16):
    return jax.ShapeDtypeStruct(dims, kind)


def picks(place_ref, dyh, dcore, relative):
    yh, x, core = place_ref[0], place_ref[1], place_ref[2]
    row = lax.broadcasted_iota(jnp.int32, (WIDE, 512), 0)
    lane = lax.broadcasted_iota(jnp.int32, (WIDE, 512), 1)
    column = row // BLOCK
    if relative:
        column = (column + x) % 4
    channel = (yh + dyh) % 2 * 256 + (core + dcore) % 2 * BLOCK + column * 64 + row % BLOCK
    return jnp.where(channel == lane, 1.0, 0.0).astype(BF16)


def regroup_kernel(place_ref, w_ref, own_ref, core_ref, far_ref):
    rows = w_ref[...]
    for block, target in enumerate((own_ref, core_ref, far_ref.at[0], far_ref.at[1])):
        order = picks(place_ref, block // 2, block % 2, True)
        picked = lax.dot_general(rows, order, NT, preferred_element_type=F32)
        target[...] = picked.astype(BF16)


def regroup(place, weight):
    rows = weight.reshape(27 * BLOCK, 512)
    one = shape((27 * BLOCK, WIDE))
    return pl.pallas_call(
        regroup_kernel,
        out_shape=(one, one, shape((2, 27 * BLOCK, WIDE))),
        in_specs=[pl.BlockSpec(memory_space=pltpu.SMEM)] + whole(1),
        out_specs=tuple(whole(3)),
        compiler_params=params(),
        cost_estimate=pl.CostEstimate(flops=2 * 864 * 512 * 512, bytes_accessed=1800000, transcendentals=0),
        name="regroup",
    )(place, rows)


def masks():
    lane = lax.broadcasted_iota(jnp.int32, (BLOCK, CELLS), 1)
    col = lane & (ROW - 1)
    one = lambda keep: jnp.where(keep, 1.0, 0.0).astype(BF16)
    return (
        one(col < ROW - 1),
        one(col > 0),
        one(lane < CELLS - ROW),
        one(lane >= ROW),
    )


def shift_plane(grads, plane, shifted, keep):
    left, right, top, bottom = keep
    for src in range(SRC):
        own_ref, rim_ref = grads[2 * src], grads[2 * src + 1]
        if plane == 0:
            mid = rim_ref[0]
        elif plane == DEPTH + 1:
            mid = rim_ref[1]
        else:
            mid = own_ref[plane - 1]
        across = (
            pltpu.roll(mid, CELLS - 1, 1) * left,
            mid,
            pltpu.roll(mid, 1, 1) * right,
        )
        for kx in range(3):
            rows = (
                pltpu.roll(across[kx], CELLS - ROW, 1) * top,
                across[kx],
                pltpu.roll(across[kx], ROW, 1) * bottom,
            )
            for ky in range(3):
                at = src * DEEP + (ky * 3 + kx) * BLOCK
                shifted[at : at + BLOCK, :] = rows[ky]


def taps_of(plane):
    return max(0, 2 - plane), min(3, DEPTH + 2 - plane)


def data_sums(grads, weights, turned, shifted, total):
    for kz in range(3):
        for src in range(SRC):
            block = weights[src][kz * DEEP : (kz + 1) * DEEP, :]
            shifted[0, src * DEEP : (src + 1) * DEEP, :WIDE] = block
        turned[kz * WIDE : (kz + 1) * WIDE, :] = shifted[0, :, :WIDE].T
    keep = masks()
    for plane in range(DEPTH + 2):
        slot = shifted.at[plane % 2]
        shift_plane(grads, plane, slot, keep)
        low, high = taps_of(plane)
        for part in range(4):
            lanes = slice(part * 256, (part + 1) * 256)
            part = lax.dot_general(
                turned[low * WIDE : high * WIDE, :], slot[:, lanes], NN, preferred_element_type=F32
            )
            for kz in range(low, high):
                at = (plane - 2 + kz) * WIDE
                piece = part[(kz - low) * WIDE : (kz - low + 1) * WIDE]
                if kz < 2:
                    piece = piece + total[at : at + WIDE, lanes]
                total[at : at + WIDE, lanes] = piece


def data_by_channel_kernel(*refs):
    grads, weights, outs = refs[:8], refs[8:12], refs[12:16]
    total = refs[-1]
    data_sums(grads, weights, *refs[16:])
    for dx in range(4):

        @pl.loop(0, DEPTH)
        def _(plane):
            at = pl.multiple_of(plane * WIDE + dx * BLOCK, BLOCK)
            outs[dx][plane] = total[pl.ds(at, BLOCK), :].astype(BF16)


def data_by_row_kernel(place_ref, *refs):
    grads, weights, outs = refs[:8], refs[8:12], refs[12:16]
    total = refs[-1]
    data_sums(grads, weights, *refs[16:])
    yh, x = place_ref[0], place_ref[1]
    for dx in range(4):

        @pl.loop(0, 2 * DEPTH)
        def _(step):
            dyh, plane = step // DEPTH, step % DEPTH
            chunk = (yh + dyh) % 2 * 4 + (x + dx) % 4
            lanes = pl.ds(pl.multiple_of(chunk * WIDE, WIDE), WIDE)
            for block in range(4):
                at = pl.multiple_of(plane * WIDE + (dx + block) % 4 * BLOCK, BLOCK)
                outs[dx][dyh, plane, block * BLOCK : (block + 1) * BLOCK] = total[pl.ds(at, BLOCK), lanes].astype(BF16)


DATA_SCRATCH = [
    pltpu.VMEM((3 * WIDE, K), BF16),
    pltpu.VMEM((2, K, CELLS), BF16),
    pltpu.VMEM((DEPTH * WIDE, CELLS), F32),
]
DATA_COST = pl.CostEstimate(flops=2 * 27 * WIDE * WIDE * DEPTH * CELLS, bytes_accessed=3500000, transcendentals=0)


def data_by_channel(grads, weights):
    return pl.pallas_call(
        data_by_channel_kernel,
        out_shape=(shape((DEPTH, BLOCK, CELLS)),) * 4,
        in_specs=whole(12),
        out_specs=tuple(whole(4)),
        scratch_shapes=DATA_SCRATCH,
        compiler_params=params(),
        cost_estimate=DATA_COST,
        name="data_by_channel",
    )(*grads, *weights)


def data_by_row(place, grads, weights):
    return pl.pallas_call(
        data_by_row_kernel,
        out_shape=(shape((2, DEPTH, WIDE, WIDE)),) * 4,
        in_specs=[pl.BlockSpec(memory_space=pltpu.SMEM)] + whole(12),
        out_specs=tuple(whole(4)),
        scratch_shapes=DATA_SCRATCH,
        compiler_params=params(),
        cost_estimate=DATA_COST,
        name="data_by_row",
    )(place, *grads, *weights)


def filter_kernel(place_ref, *refs):
    grads, sources, out_ref = refs[:8], refs[8:9], refs[9]
    stacked, shifted, total = refs[10:]
    for x in range(4):
        for plane in range(DEPTH):
            at = plane * WIDE + x * BLOCK
            stacked[at : at + BLOCK, :] = sources[0][x, plane]

    keep = masks()
    for plane in range(DEPTH + 2):
        slot = shifted.at[plane % 2]
        shift_plane(grads, plane, slot, keep)
        low, high = taps_of(plane)
        first = plane - 2 + low
        for src in range(SRC):
            part = lax.dot_general(
                slot[src * DEEP : (src + 1) * DEEP, :],
                stacked[first * WIDE : (first + high - low) * WIDE, :],
                NT,
                preferred_element_type=F32,
            )
            for kz in range(low, high):
                piece = part[:, (kz - low) * WIDE : (kz - low + 1) * WIDE]
                lanes = slice(kz * WIDE, (kz + 1) * WIDE)
                if plane != 2 - kz:
                    piece = piece + total[src, :, lanes]
                total[src, :, lanes] = piece

    upper = lax.broadcasted_iota(jnp.int32, (18, 8, 3 * WIDE), 1) < 4

    for z in range(4):
        rows = total[...].reshape(18, 2, 4, 8, 3 * WIDE)
        one, two = rows[:, 0, z], rows[:, 1, z]
        low = jnp.where(upper, one, pltpu.roll(two, 4, 1))
        high = jnp.where(upper, pltpu.roll(one, 4, 1), two)
        out_ref[2 * z] = low.reshape(18 * 8, 3 * WIDE).astype(BF16)
        out_ref[2 * z + 1] = high.reshape(18 * 8, 3 * WIDE).astype(BF16)


def filter_sums(place, grads, sources):
    return pl.pallas_call(
        filter_kernel,
        out_shape=shape((8, SRC * TAPS * 4, 3 * WIDE)),
        in_specs=[pl.BlockSpec(memory_space=pltpu.SMEM)] + whole(9),
        out_specs=whole(1)[0],
        scratch_shapes=[
            pltpu.VMEM((DEPTH * WIDE, CELLS), BF16),
            pltpu.VMEM((2, K, CELLS), BF16),
            pltpu.VMEM((SRC, DEEP, 3 * WIDE), F32),
        ],
        compiler_params=params(),
        cost_estimate=DATA_COST,
        name="filter_sums",
    )(place, *grads, sources)


def gather_outputs(own):
    core = from_ahead(own, "core", 1)
    far = from_ahead(own, "yh", 1)
    return own, core, far, from_ahead(far, "core", 1)


def sum_ahead(blocks, axis):
    total = blocks[0].astype(F32)
    for d in range(1, 4):
        total = total + from_ahead(blocks[d], axis, -d).astype(F32)
    return total


def gather_weight(place, weight):
    own, core, far = regroup(place, weight)
    far = from_ahead(far, "yh", 1)
    return own, from_ahead(core, "core", 1), far[0], from_ahead(far[1], "core", 1)


def gather_grads(own):
    low = lax.ppermute(own[DEPTH - 1 :], GZ, [(i, i + 1) for i in range(7)])
    high = lax.ppermute(own[:1], GZ, [(i + 1, i) for i in range(7)])
    rim = jnp.concatenate([low, high], axis=0)
    grads = []
    for a, b in zip(gather_outputs(own), gather_outputs(rim)):
        grads += [a, b]
    return grads


def place_filters_kernel(place_ref, factor_ref, a, b, c, d, out_ref):
    for src, ref in enumerate((a, b, c, d)):
        order = picks(place_ref, src // 2, src % 2, False)
        for kz in range(3):
            part = lax.dot_general(
                ref[:, kz * WIDE : (kz + 1) * WIDE], order, NN, preferred_element_type=F32
            )
            if src:
                part = part + out_ref[kz]
            if src == 3:
                part = part * factor_ref[0]
            out_ref[kz] = part


def finish_filters(place, sums, factor):
    count = len(sums)
    rows = jnp.stack([one.reshape(2, 2, TAPS * 4, 3 * WIDE) for one in sums], axis=2)
    far = from_ahead(rows[1], "yh", 1)
    got = from_ahead(jnp.stack([rows[0, 1], far[1]]), "core", 1)
    blocks = [rows[0, 0], got[0], far[0], got[1]]
    out = pl.pallas_call(
        place_filters_kernel,
        out_shape=shape((3, count * TAPS * 4, 512), F32),
        in_specs=[pl.BlockSpec(memory_space=pltpu.SMEM)] * 2 + whole(4),
        out_specs=whole(1)[0],
        compiler_params=params(),
        name="place_filters",
    )(place, factor.reshape(1), *[one.reshape(count * TAPS * 4, 3 * WIDE) for one in blocks])
    out = out.reshape(3, count, 3, 3, 4, 512)
    return [out[:, i] for i in range(count)]


def place_kernel(place_ref, a, b, c, d, out_ref, rows):
    start = pl.multiple_of(place_ref[2] * 64, 64)
    orders = [picks(place_ref, src // 2, src % 2, True) for src in range(SRC)]
    for plane in range(DEPTH):
        total = None
        for order, ref in zip(orders, (a, b, c, d)):
            part = lax.dot_general(ref[plane].T, order, NN, preferred_element_type=F32)
            total = part if total is None else total + part
        rows[...] = total
        out_ref[plane] = rows[pl.ds(start, 64), :].astype(BF16)


def finish_image(parts, place):
    part = sum_ahead(parts, "x").astype(BF16)
    near = part[0]
    far = from_ahead(part[1], "yh", 1)
    near_got = from_ahead(near, "core", 1)
    far_got = from_ahead(far, "core", 1)
    out = pl.pallas_call(
        place_kernel,
        out_shape=shape((DEPTH, 64, 512)),
        in_specs=[pl.BlockSpec(memory_space=pltpu.SMEM)] + whole(4),
        out_specs=whole(1)[0],
        scratch_shapes=[pltpu.VMEM((WIDE, 512), F32)],
        compiler_params=params(),
        name="place",
    )(place, near, near_got, far, far_got)
    return out.reshape(DEPTH, 2, ROW, 512)


def after(place, done):
    return lax.optimization_barrier((place, done))[0]


def body(inputs, preact, cotangent, weight1, weight2):
    place = jnp.stack([lax.axis_index(a) for a in AF]).astype(jnp.int32)
    factor = 1.0 / jnp.sqrt(F32(32 * CELLS))

    cot = cotangent.transpose(1, 0, 2)
    weights2 = gather_weight(place, weight2)
    grads2 = gather_grads(cot)
    pre = preact.transpose(1, 0, 2)
    hidden = lax.all_gather(jnp.maximum(pre, jnp.zeros((), BF16)), "x", axis=0)
    sources = lax.all_gather(inputs.transpose(1, 0, 2), "x", axis=0)

    unit_parts = data_by_channel(grads2, weights2)
    later = after(place, unit_parts[0])
    weights1 = gather_weight(later, weight1)
    filter2_parts = filter_sums(later, grads2, hidden)
    filter2_sum = lax.psum_scatter(filter2_parts, GZ, scatter_dimension=0)
    unit = sum_ahead(unit_parts, "x")
    preact_grad = jnp.where(pre > 0, unit, 0.0).astype(BF16)
    grads1 = gather_grads(preact_grad)
    filter1_parts = filter_sums(place, grads1, sources)
    filter1_sum = lax.psum_scatter(filter1_parts, GZ, scatter_dimension=0)
    image_parts = data_by_row(after(place, filter1_parts), grads1, weights1)
    input_grad = finish_image(image_parts, place)
    filter1_grad, filter2_grad = finish_filters(place, [filter1_sum, filter2_sum], factor)
    return input_grad, filter1_grad, filter2_grad


def solution(mesh):
    fine = Mesh(mesh.devices.reshape(2, 4, 2, 4, 2), AF + GZ)
    placed = (
        P(AF, GZ, None),
        P(AF, GZ, None),
        P(AF, GZ, None),
        P(None, None, None, AF, None),
        P(None, None, None, AF, None),
    )
    return jax.shard_map(
        body,
        mesh=fine,
        in_specs=placed,
        out_specs=(
            P(GZ, AF, None, None),
            P(None, None, None, AF + GZ, None),
            P(None, None, None, AF + GZ, None),
        ),
        check_vma=False,
    )
```

profile of v0, /device:TPU:1, one launch (start us, length us, event | category | flops | bytes accessed | tf_op | source)
XLA Modules:
  0.0 204.2 jit_solution(388479907517471898)
XLA Ops:
  7.2 1.7 copy.37
  11.9 3.8 %collective-permute-start.9 = (bf16[2,864,128]{2,1,0:T(8,128)(2,1)S(1)}, bf16[2,864,128]{2,1,0:T(8,128)(2,1)S(1)}, u32[]{:S(2)}, u32[]{:S(2)}) collective-permute-start(bf16[2,864,128]{2,1,0:T(8,128)(2,1)S(1)} %get-tuple-element.21), channel_id=1, source_target_pairs={{0,64},{64,0},{1,65},{65,1},{2,66},{66,2},{3,67},{67,3},{4,68},{68... | collective-permute-start | bytes 1327112 | tf_op jit(solution)/shard_map/ppermute | solution.py:40
  15.9 2.3 %collective-permute-start = (bf16[1,32,1024]{2,1,0:T(8,128)(2,1)S(1)}, bf16[1,32,1024]{2,1,0:T(8,128)(2,1)S(1)}, u32[]{:S(2)}, u32[]{:S(2)}) collective-permute-start(bf16[1,32,1024]{2,1,0:T(8,128)(2,1)S(1)} %get-tuple-element.46), channel_id=1, source_target_pairs={{0,1},{1,2},{2,3},{3,4},{4,5},{5,6},{6,7},{8,9},{9,10},{10,11},{11... | collective-permute-start | bytes 196616 | tf_op jit(solution)/shard_map/ppermute | solution.py:285
  22.6 3.4 %collective-permute-done = bf16[1,32,1024]{2,1,0:T(8,128)(2,1)S(1)} collective-permute-done((bf16[1,32,1024]{2,1,0:T(8,128)(2,1)S(1)}, bf16[1,32,1024]{2,1,0:T(8,128)(2,1)S(1)}, u32[]{:S(2)}, u32[]{:S(2)}) %collective-permute-start) | collective-permute-done | bytes 65568 | tf_op jit(solution)/shard_map/ppermute | solution.py:285
  26.0 2.7 %collective-permute-start.8 = (bf16[864,128]{1,0:T(8,128)(2,1)S(1)}, bf16[864,128]{1,0:T(8,128)(2,1)S(1)}, u32[]{:S(2)}, u32[]{:S(2)}) collective-permute-start(bf16[864,128]{1,0:T(8,128)(2,1)S(1)} %get-tuple-element.20), channel_id=1, source_target_pairs={{0,8},{8,0},{1,9},{9,1},{2,10},{10,2},{3,11},{11,3},{4,12},{12,4},... | collective-permute-start | bytes 663560 | tf_op jit(solution)/shard_map/ppermute | solution.py:40
  28.7 5.6 %collective-permute-done.1 = bf16[1,32,1024]{2,1,0:T(8,128)(2,1)S(1)} collective-permute-done((bf16[1,32,1024]{2,1,0:T(8,128)(2,1)S(1)}, bf16[1,32,1024]{2,1,0:T(8,128)(2,1)S(1)}, u32[]{:S(2)}, u32[]{:S(2)}) %collective-permute-start.1) | collective-permute-done | bytes 65568 | tf_op jit(solution)/shard_map/ppermute | solution.py:286
  35.8 1.7 collective-permute-start.3
  37.7 1.9 collective-permute-done.5.refs_5_
  39.6 2.6 %collective-permute-start.10 = (bf16[864,128]{1,0:T(8,128)(2,1)S(1)}, bf16[864,128]{1,0:T(8,128)(2,1)S(1)}, u32[]{:S(2)}, u32[]{:S(2)}) collective-permute-start(bf16[864,128]{1,0:T(8,128)(2,1)S(1)} %get-tuple-element.39), channel_id=1, source_target_pairs={{0,8},{8,0},{1,9},{9,1},{2,10},{10,2},{3,11},{11,3},{4,12},{12,4},... | collective-permute-start | bytes 663560 | tf_op jit(solution)/shard_map/ppermute | solution.py:40
  43.6 6.9 %data_by_channel.1 = (bf16[4,32,1024]{2,1,0:T(8,128)(2,1)S(1)}, bf16[4,32,1024]{2,1,0:T(8,128)(2,1)S(1)}, bf16[4,32,1024]{2,1,0:T(8,128)(2,1)S(1)}, bf16[4,32,1024]{2,1,0:T(8,128)(2,1)S(1)}) custom-call(bf16[4,32,1024]{2,1,0:T(8,128)(2,1)S(1)} %bitcast.55, bf16[2,32,1024]{2,1,0:T(8,128)(2,1)S(1)} %constant_dynamic-update-slice_fusion.refs_1_, ...), custom_call_target="tpu_custom_call" | custom-call | flops 3623878656 | bytes 3500000 | tf_op jit(solution)/shard_map/data_by_channel/pallas_call | solution.py:184
  51.8 2.5 %collective-permute-start.12 = (bf16[4,32,1024]{2,1,0:T(8,128)(2,1)S(1)}, bf16[4,32,1024]{2,1,0:T(8,128)(2,1)S(1)}, u32[]{:S(2)}, u32[]{:S(2)}) collective-permute-start(bf16[4,32,1024]{2,1,0:T(8,128)(2,1)S(1)} %get-tuple-element.24), channel_id=1, source_target_pairs={{0,32},{16,48},{32,0},{48,16},{1,33},{17,49},{33,1},{49,17},{2,34}... | collective-permute-start | bytes 786440 | tf_op jit(solution)/shard_map/ppermute | solution.py:40
  56.2 3.1 %collective-permute-done.11 = bf16[4,32,1024]{2,1,0:T(8,128)(2,1)S(1)} collective-permute-done((bf16[4,32,1024]{2,1,0:T(8,128)(2,1)S(1)}, bf16[4,32,1024]{2,1,0:T(8,128)(2,1)S(1)}, u32[]{:S(2)}, u32[]{:S(2)}) %collective-permute-start.11) | collective-permute-done | bytes 262176 | tf_op jit(solution)/shard_map/ppermute | solution.py:40
  59.4 6.6 %collective-permute-done.12 = bf16[4,32,1024]{2,1,0:T(8,128)(2,1)S(1)} collective-permute-done((bf16[4,32,1024]{2,1,0:T(8,128)(2,1)S(1)}, bf16[4,32,1024]{2,1,0:T(8,128)(2,1)S(1)}, u32[]{:S(2)}, u32[]{:S(2)}) %collective-permute-start.12) | collective-permute-done | bytes 262176 | tf_op jit(solution)/shard_map/ppermute | solution.py:40
  66.3 4.3 %collective-permute-start.14 = (bf16[1,32,1024]{2,1,0:T(8,128)(2,1)S(1)}, bf16[1,32,1024]{2,1,0:T(8,128)(2,1)S(1)}, u32[]{:S(2)}, u32[]{:S(2)}) collective-permute-start(bf16[1,32,1024]{2,1,0:T(8,128)(2,1)S(1)} %get-tuple-element.44), channel_id=1, source_target_pairs={{0,1},{1,2},{2,3},{3,4},{4,5},{5,6},{6,7},{8,9},{9,10},{10,11},{11... | collective-permute-start | bytes 196616 | tf_op jit(solution)/shard_map/ppermute | solution.py:285
  74.0 5.8 %collective-permute-done.15 = bf16[1,32,1024]{2,1,0:T(8,128)(2,1)S(1)} collective-permute-done((bf16[1,32,1024]{2,1,0:T(8,128)(2,1)S(1)}, bf16[1,32,1024]{2,1,0:T(8,128)(2,1)S(1)}, u32[]{:S(2)}, u32[]{:S(2)}) %collective-permute-start.15) | collective-permute-done | bytes 65568 | tf_op jit(solution)/shard_map/ppermute | solution.py:286
  81.5 2.3 %collective-permute-start.20 = (bf16[4,32,1024]{2,1,0:T(8,128)(2,1)S(1)}, bf16[4,32,1024]{2,1,0:T(8,128)(2,1)S(1)}, u32[]{:S(2)}, u32[]{:S(2)}) collective-permute-start(bf16[4,32,1024]{2,1,0:T(8,128)(2,1)S(1)} %collective-permute-done.18.refs_4_), channel_id=1, source_target_pairs={{0,8},{8,0},{1,9},{9,1},{2,10},{10,2},{3,11},{11,3},{4,12},{12,4},... | collective-permute-start | bytes 786440 | tf_op jit(solution)/shard_map/ppermute | solution.py:40
  85.2 2.7 %collective-permute-start.21 = (bf16[2,32,1024]{2,1,0:T(8,128)(2,1)S(1)}, bf16[2,32,1024]{2,1,0:T(8,128)(2,1)S(1)}, u32[]{:S(2)}, u32[]{:S(2)}) collective-permute-start(bf16[2,32,1024]{2,1,0:T(8,128)(2,1)S(1)} %collective-permute-done.19.refs_5_), channel_id=1, source_target_pairs={{0,8},{8,0},{1,9},{9,1},{2,10},{10,2},{3,11},{11,3},{4,12},{12,4},... | collective-permute-start | bytes 393224 | tf_op jit(solution)/shard_map/ppermute | solution.py:40
  90.0 8.4 %filter_sums.2 = bf16[8,144,384]{2,1,0:T(8,128)(2,1)} custom-call(s32[3]{0:T(128)S(1)} %pad_add_fusion.place_ref, bf16[4,32,1024]{2,1,0:T(8,128)(2,1)S(1)} %select_convert_fusion.refs_0_, bf16[2,32,1024]{2,1,0:T(8,128)(2,1)S(1)} %constant_dynamic-update-slice_fusion.2.refs_1_, bf16[4,32,1024]{2,1,0:T(8,128)(2,1)S(1)} %collective-permute-done.16.refs_2_, ...), custom_call_target="tpu_custom_call" | custom-call | flops 3623878656 | bytes 3500000 | tf_op jit(solution)/shard_map/filter_sums/pallas_call | solution.py:249
  104.7 2.1 %collective-permute-start.23 = (bf16[2,864,128]{2,1,0:T(8,128)(2,1)S(1)}, bf16[2,864,128]{2,1,0:T(8,128)(2,1)}, u32[]{:S(2)}, u32[]{:S(2)}) collective-permute-start(bf16[2,864,128]{2,1,0:T(8,128)(2,1)S(1)} %get-tuple-element.30), channel_id=1, source_target_pairs={{0,64},{64,0},{1,65},{65,1},{2,66},{66,2},{3,67},{67,3},{4,68},{68... | collective-permute-start | bytes 1327112 | tf_op jit(solution)/shard_map/ppermute | solution.py:40
  110.5 8.4 %filter_sums.3 = bf16[8,144,384]{2,1,0:T(8,128)(2,1)} custom-call(s32[3]{0:T(128)S(1)} %pad_add_fusion.place_ref, bf16[4,32,1024]{2,1,0:T(8,128)(2,1)S(1)} %bitcast.56, bf16[2,32,1024]{2,1,0:T(8,128)(2,1)S(1)} %constant_dynamic-update-slice_fusion.refs_1_, bf16[4,32,1024]{2,1,0:T(8,128)(2,1)S(1)} %collective-permute-done.2.refs_2_, ...), custom_call_target="tpu_custom_call" | custom-call | flops 3623878656 | bytes 3500000 | tf_op jit(solution)/shard_map/filter_sums/pallas_call | solution.py:249
  121.8 2.9 %collective-permute-start.24 = (bf16[864,128]{1,0:T(8,128)(2,1)S(1)}, bf16[864,128]{1,0:T(8,128)(2,1)S(1)}, u32[]{:S(2)}, u32[]{:S(2)}) collective-permute-start(bf16[864,128]{1,0:T(8,128)(2,1)S(1)} %get-tuple-element.37), channel_id=1, source_target_pairs={{0,8},{8,0},{1,9},{9,1},{2,10},{10,2},{3,11},{11,3},{4,12},{12,4},... | collective-permute-start | bytes 663560 | tf_op jit(solution)/shard_map/ppermute | solution.py:40
  125.8 8.1 %data_by_row.1 = (bf16[2,4,128,128]{3,2,1,0:T(8,128)(2,1)S(1)}, bf16[2,4,128,128]{3,2,1,0:T(8,128)(2,1)S(1)}, bf16[2,4,128,128]{3,2,1,0:T(8,128)(2,1)S(1)}, bf16[2,4,128,128]{3,2,1,0:T(8,128)(2,1)S(1)}) custom-call(s32[3]{0:T(128)S(1)} %pad_add_fusion.place_ref, bf16[4,32,1024]{2,1,0:T(8,128)(2,1)S(1)} %select_convert_fusion.refs_0_, ...), custom_call_target="tpu_custom_call" | custom-call | flops 3623878656 | bytes 3500000 | tf_op jit(solution)/shard_map/data_by_row/pallas_call | solution.py:197
  134.9 2.9 %collective-permute-start.26 = (bf16[2,4,128,128]{3,2,1,0:T(8,128)(2,1)S(1)}, bf16[2,4,128,128]{3,2,1,0:T(8,128)(2,1)S(1)}, u32[]{:S(2)}, u32[]{:S(2)}) collective-permute-start(bf16[2,4,128,128]{3,2,1,0:T(8,128)(2,1)S(1)} %get-tuple-element.33), channel_id=1, source_target_pairs={{0,32},{16,48},{32,0},{48,16},{1,33},{17,49},{33,1},{49,17},{2,34}... | collective-permute-start | bytes 786440 | tf_op jit(solution)/shard_map/ppermute | solution.py:40
  138.1 4.6 %collective-permute-done.25 = bf16[2,4,128,128]{3,2,1,0:T(8,128)(2,1)S(1)} collective-permute-done((bf16[2,4,128,128]{3,2,1,0:T(8,128)(2,1)S(1)}, bf16[2,4,128,128]{3,2,1,0:T(8,128)(2,1)S(1)}, u32[]{:S(2)}, u32[]{:S(2)}) %collective-permute-start.25) | collective-permute-done | bytes 262176 | tf_op jit(solution)/shard_map/ppermute | solution.py:40
  142.7 6.8 %collective-permute-done.26 = bf16[2,4,128,128]{3,2,1,0:T(8,128)(2,1)S(1)} collective-permute-done((bf16[2,4,128,128]{3,2,1,0:T(8,128)(2,1)S(1)}, bf16[2,4,128,128]{3,2,1,0:T(8,128)(2,1)S(1)}, u32[]{:S(2)}, u32[]{:S(2)}) %collective-permute-start.26) | collective-permute-done | bytes 262176 | tf_op jit(solution)/shard_map/ppermute | solution.py:40
  149.7 3.6 %collective-permute-start.29 = (bf16[4,128,128]{2,1,0:T(8,128)(2,1)S(1)}, bf16[4,128,128]{2,1,0:T(8,128)(2,1)S(1)}, u32[]{:S(2)}, u32[]{:S(2)}) collective-permute-start(bf16[4,128,128]{2,1,0:T(8,128)(2,1)S(1)} %get-tuple-element.41), channel_id=1, source_target_pairs={{0,64},{64,0},{1,65},{65,1},{2,66},{66,2},{3,67},{67,3},{4,68},{68... | collective-permute-start | bytes 393224 | tf_op jit(solution)/shard_map/ppermute | solution.py:40
  154.8 2.9 %collective-permute-done.29.c = bf16[4,128,128]{2,1,0:T(8,128)(2,1)S(1)} collective-permute-done((bf16[4,128,128]{2,1,0:T(8,128)(2,1)S(1)}, bf16[4,128,128]{2,1,0:T(8,128)(2,1)S(1)}, u32[]{:S(2)}, u32[]{:S(2)}) %collective-permute-start.29) | collective-permute-done | bytes 131104 | tf_op jit(solution)/shard_map/ppermute | solution.py:40
  159.8 20.1 %reduce-scatter.5.cloned.1.call-done = bf16[1,144,384]{2,1,0:T(8,128)(2,1)} async-done(((bf16[8,144,384]{2,1,0:T(8,128)(2,1)}), bf16[1,144,384]{2,1,0:T(8,128)(2,1)}) %reduce-scatter.5.cloned.1.call-update) | async-done | bytes 110608 | tf_op jit(solution)/shard_map/reduce_scatter | solution.py:375
  180.8 2.6 %collective-permute-start.31 = (bf16[2,2,36,384]{3,2,0,1:T(8,128)(2,1)S(1)}, bf16[2,2,36,384]{3,2,0,1:T(8,128)(2,1)S(1)}, u32[]{:S(2)}, u32[]{:S(2)}) collective-permute-start(bf16[2,2,36,384]{3,2,0,1:T(8,128)(2,1)S(1)} %slice_bitcast_fusion.8), channel_id=1, source_target_pairs={{0,64},{64,0},{1,65},{65,1},{2,66},{66,2},{3,67},{67,3},{4,68},{68... | collective-permute-start | bytes 331784 | tf_op jit(solution)/shard_map/ppermute | solution.py:40
  183.4 2.7 %collective-permute-done.31 = bf16[2,2,36,384]{3,2,0,1:T(8,128)(2,1)S(1)} collective-permute-done((bf16[2,2,36,384]{3,2,0,1:T(8,128)(2,1)S(1)}, bf16[2,2,36,384]{3,2,0,1:T(8,128)(2,1)S(1)}, u32[]{:S(2)}, u32[]{:S(2)}) %collective-permute-start.31) | collective-permute-done | bytes 110624 | tf_op jit(solution)/shard_map/ppermute | solution.py:40
  186.2 7.4 %collective-permute-start.32 = (bf16[2,2,36,384]{3,2,0,1:T(8,128)(2,1)S(1)}, bf16[2,2,36,384]{3,2,0,1:T(8,128)(2,1)S(1)}, u32[]{:S(2)}, u32[]{:S(2)}) collective-permute-start(bf16[2,2,36,384]{3,2,0,1:T(8,128)(2,1)S(1)} %pad_maximum_fusion), channel_id=1, source_target_pairs={{0,8},{8,0},{1,9},{9,1},{2,10},{10,2},{3,11},{11,3},{4,12},{12,4},... | collective-permute-start | bytes 331784 | tf_op jit(solution)/shard_map/ppermute | solution.py:40
  193.6 2.0 place.1
  (132 shorter events, 44.5 us)
Async XLA Ops:
  7.2 81.7 %all-gather.5.cloned.1.call-start = ((), (), s32[]{:S(2)}) async-start(), calls=%async_computation.4 | async-start | bytes 1310720 | tf_op jit(solution)/shard_map/all_gather | solution.py:369
  9.0 98.5 %all-gather.7.cloned.1.call-start = ((), (), s32[]{:S(2)}) async-start(), calls=%async_computation.5 | async-start | bytes 1310720 | tf_op jit(solution)/shard_map/all_gather | solution.py:368
  11.9 25.6 %collective-permute-start.9 = (bf16[2,864,128]{2,1,0:T(8,128)(2,1)S(1)}, bf16[2,864,128]{2,1,0:T(8,128)(2,1)S(1)}, u32[]{:S(2)}, u32[]{:S(2)}) collective-permute-start(bf16[2,864,128]{2,1,0:T(8,128)(2,1)S(1)} %get-tuple-element.21), channel_id=1, source_target_pairs={{0,64},{64,0},{1,65},{65,1},{2,66},{66,2},{3,67},{67,3},{4,68},{68... | collective-permute-start | bytes 1327112 | tf_op jit(solution)/shard_map/ppermute | solution.py:40
  15.9 10.1 %collective-permute-start = (bf16[1,32,1024]{2,1,0:T(8,128)(2,1)S(1)}, bf16[1,32,1024]{2,1,0:T(8,128)(2,1)S(1)}, u32[]{:S(2)}, u32[]{:S(2)}) collective-permute-start(bf16[1,32,1024]{2,1,0:T(8,128)(2,1)S(1)} %get-tuple-element.46), channel_id=1, source_target_pairs={{0,1},{1,2},{2,3},{3,4},{4,5},{5,6},{6,7},{8,9},{9,10},{10,11},{11... | collective-permute-start | bytes 196616 | tf_op jit(solution)/shard_map/ppermute | solution.py:285
  18.2 17.6 %collective-permute-start.4 = (bf16[4,32,1024]{2,1,0:T(8,128)(2,1)S(1)}, bf16[4,32,1024]{2,1,0:T(8,128)(2,1)S(1)}, u32[]{:S(2)}, u32[]{:S(2)}) collective-permute-start(bf16[4,32,1024]{2,1,0:T(8,128)(2,1)S(1)} %bitcast.53), channel_id=1, source_target_pairs={{0,64},{64,0},{1,65},{65,1},{2,66},{66,2},{3,67},{67,3},{4,68},{68... | collective-permute-start | bytes 786440 | tf_op jit(solution)/shard_map/ppermute | solution.py:40
  19.8 22.5 %collective-permute-start.2 = (bf16[4,32,1024]{2,1,0:T(8,128)(2,1)S(1)}, bf16[4,32,1024]{2,1,0:T(8,128)(2,1)S(1)}, u32[]{:S(2)}, u32[]{:S(2)}) collective-permute-start(bf16[4,32,1024]{2,1,0:T(8,128)(2,1)S(1)} %bitcast.54), channel_id=1, source_target_pairs={{0,8},{8,0},{1,9},{9,1},{2,10},{10,2},{3,11},{11,3},{4,12},{12,4},... | collective-permute-start | bytes 786440 | tf_op jit(solution)/shard_map/ppermute | solution.py:40
  21.3 12.9 %collective-permute-start.1 = (bf16[1,32,1024]{2,1,0:T(8,128)(2,1)S(1)}, bf16[1,32,1024]{2,1,0:T(8,128)(2,1)S(1)}, u32[]{:S(2)}, u32[]{:S(2)}) collective-permute-start(bf16[1,32,1024]{2,1,0:T(8,128)(2,1)S(1)} %get-tuple-element.45), channel_id=1, source_target_pairs={{1,0},{2,1},{3,2},{4,3},{5,4},{6,5},{7,6},{9,8},{10,9},{11,10},{12... | collective-permute-start | bytes 196616 | tf_op jit(solution)/shard_map/ppermute | solution.py:286
  26.0 16.3 %collective-permute-start.8 = (bf16[864,128]{1,0:T(8,128)(2,1)S(1)}, bf16[864,128]{1,0:T(8,128)(2,1)S(1)}, u32[]{:S(2)}, u32[]{:S(2)}) collective-permute-start(bf16[864,128]{1,0:T(8,128)(2,1)S(1)} %get-tuple-element.20), channel_id=1, source_target_pairs={{0,8},{8,0},{1,9},{9,1},{2,10},{10,2},{3,11},{11,3},{4,12},{12,4},... | collective-permute-start | bytes 663560 | tf_op jit(solution)/shard_map/ppermute | solution.py:40
  34.3 5.3 %collective-permute-start.5 = (bf16[2,32,1024]{2,1,0:T(8,128)(2,1)S(1)}, bf16[2,32,1024]{2,1,0:T(8,128)(2,1)S(1)}, u32[]{:S(2)}, u32[]{:S(2)}) collective-permute-start(bf16[2,32,1024]{2,1,0:T(8,128)(2,1)S(1)} %constant_dynamic-update-slice_fusion.refs_1_), channel_id=1, source_target_pairs={{0,64},{64,0},{1,65},{65,1},{2,66},{66,2},{3,67},{67,3},{4,68},{68... | collective-permute-start | bytes 393224 | tf_op jit(solution)/shard_map/ppermute | solution.py:40
  35.8 6.4 %collective-permute-start.3 = (bf16[2,32,1024]{2,1,0:T(8,128)(2,1)S(1)}, bf16[2,32,1024]{2,1,0:T(8,128)(2,1)S(1)}, u32[]{:S(2)}, u32[]{:S(2)}) collective-permute-start(bf16[2,32,1024]{2,1,0:T(8,128)(2,1)S(1)} %constant_dynamic-update-slice_fusion.refs_1_), channel_id=1, source_target_pairs={{0,8},{8,0},{1,9},{9,1},{2,10},{10,2},{3,11},{11,3},{4,12},{12,4},... | collective-permute-start | bytes 393224 | tf_op jit(solution)/shard_map/ppermute | solution.py:40
  37.5 6.0 %collective-permute-start.6 = (bf16[4,32,1024]{2,1,0:T(8,128)(2,1)S(1)}, bf16[4,32,1024]{2,1,0:T(8,128)(2,1)S(1)}, u32[]{:S(2)}, u32[]{:S(2)}) collective-permute-start(bf16[4,32,1024]{2,1,0:T(8,128)(2,1)S(1)} %collective-permute-done.4.refs_4_), channel_id=1, source_target_pairs={{0,8},{8,0},{1,9},{9,1},{2,10},{10,2},{3,11},{11,3},{4,12},{12,4},... | collective-permute-start | bytes 786440 | tf_op jit(solution)/shard_map/ppermute | solution.py:40
  50.5 8.9 %collective-permute-start.11 = (bf16[4,32,1024]{2,1,0:T(8,128)(2,1)S(1)}, bf16[4,32,1024]{2,1,0:T(8,128)(2,1)S(1)}, u32[]{:S(2)}, u32[]{:S(2)}) collective-permute-start(bf16[4,32,1024]{2,1,0:T(8,128)(2,1)S(1)} %get-tuple-element.23), channel_id=1, source_target_pairs={{0,16},{16,32},{32,48},{48,0},{1,17},{17,33},{33,49},{49,1},{2,18}... | collective-permute-start | bytes 786440 | tf_op jit(solution)/shard_map/ppermute | solution.py:40
  51.8 14.3 %collective-permute-start.12 = (bf16[4,32,1024]{2,1,0:T(8,128)(2,1)S(1)}, bf16[4,32,1024]{2,1,0:T(8,128)(2,1)S(1)}, u32[]{:S(2)}, u32[]{:S(2)}) collective-permute-start(bf16[4,32,1024]{2,1,0:T(8,128)(2,1)S(1)} %get-tuple-element.24), channel_id=1, source_target_pairs={{0,32},{16,48},{32,0},{48,16},{1,33},{17,49},{33,1},{49,17},{2,34}... | collective-permute-start | bytes 786440 | tf_op jit(solution)/shard_map/ppermute | solution.py:40
  54.2 11.8 %collective-permute-start.13 = (bf16[4,32,1024]{2,1,0:T(8,128)(2,1)S(1)}, bf16[4,32,1024]{2,1,0:T(8,128)(2,1)S(1)}, u32[]{:S(2)}, u32[]{:S(2)}) collective-permute-start(bf16[4,32,1024]{2,1,0:T(8,128)(2,1)S(1)} %get-tuple-element.25), channel_id=1, source_target_pairs={{0,48},{16,0},{32,16},{48,32},{1,49},{17,1},{33,17},{49,33},{2,50}... | collective-permute-start | bytes 786440 | tf_op jit(solution)/shard_map/ppermute | solution.py:40
  56.2 102.6 %reduce-scatter.3.cloned.1.call-start = ((), (), s32[]{:S(2)}) async-start(), calls=%async_computation.2 | async-start | bytes 995328 | tf_op jit(solution)/shard_map/reduce_scatter | solution.py:380
  66.3 7.7 %collective-permute-start.14 = (bf16[1,32,1024]{2,1,0:T(8,128)(2,1)S(1)}, bf16[1,32,1024]{2,1,0:T(8,128)(2,1)S(1)}, u32[]{:S(2)}, u32[]{:S(2)}) collective-permute-start(bf16[1,32,1024]{2,1,0:T(8,128)(2,1)S(1)} %get-tuple-element.44), channel_id=1, source_target_pairs={{0,1},{1,2},{2,3},{3,4},{4,5},{5,6},{6,7},{8,9},{9,10},{10,11},{11... | collective-permute-start | bytes 196616 | tf_op jit(solution)/shard_map/ppermute | solution.py:285
  70.6 10.9 %collective-permute-start.18 = (bf16[4,32,1024]{2,1,0:T(8,128)(2,1)S(1)}, bf16[4,32,1024]{2,1,0:T(8,128)(2,1)S(1)}, u32[]{:S(2)}, u32[]{:S(2)}) collective-permute-start(bf16[4,32,1024]{2,1,0:T(8,128)(2,1)S(1)} %select_convert_fusion.refs_0_), channel_id=1, source_target_pairs={{0,64},{64,0},{1,65},{65,1},{2,66},{66,2},{3,67},{67,3},{4,68},{68... | collective-permute-start | bytes 786440 | tf_op jit(solution)/shard_map/ppermute | solution.py:40
  71.0 16.8 %collective-permute-start.16 = (bf16[4,32,1024]{2,1,0:T(8,128)(2,1)S(1)}, bf16[4,32,1024]{2,1,0:T(8,128)(2,1)S(1)}, u32[]{:S(2)}, u32[]{:S(2)}) collective-permute-start(bf16[4,32,1024]{2,1,0:T(8,128)(2,1)S(1)} %select_convert_fusion.refs_0_), channel_id=1, source_target_pairs={{0,8},{8,0},{1,9},{9,1},{2,10},{10,2},{3,11},{11,3},{4,12},{12,4},... | collective-permute-start | bytes 786440 | tf_op jit(solution)/shard_map/ppermute | solution.py:40
  72.7 7.1 %collective-permute-start.15 = (bf16[1,32,1024]{2,1,0:T(8,128)(2,1)S(1)}, bf16[1,32,1024]{2,1,0:T(8,128)(2,1)S(1)}, u32[]{:S(2)}, u32[]{:S(2)}) collective-permute-start(bf16[1,32,1024]{2,1,0:T(8,128)(2,1)S(1)} %get-tuple-element.43), channel_id=1, source_target_pairs={{1,0},{2,1},{3,2},{4,3},{5,4},{6,5},{7,6},{9,8},{10,9},{11,10},{12... | collective-permute-start | bytes 196616 | tf_op jit(solution)/shard_map/ppermute | solution.py:286
  79.8 5.3 %collective-permute-start.19 = (bf16[2,32,1024]{2,1,0:T(8,128)(2,1)S(1)}, bf16[2,32,1024]{2,1,0:T(8,128)(2,1)S(1)}, u32[]{:S(2)}, u32[]{:S(2)}) collective-permute-start(bf16[2,32,1024]{2,1,0:T(8,128)(2,1)S(1)} %constant_dynamic-update-slice_fusion.2.refs_1_), channel_id=1, source_target_pairs={{0,64},{64,0},{1,65},{65,1},{2,66},{66,2},{3,67},{67,3},{4,68},{68... | collective-permute-start | bytes 393224 | tf_op jit(solution)/shard_map/ppermute | solution.py:40
  81.5 7.3 %collective-permute-start.20 = (bf16[4,32,1024]{2,1,0:T(8,128)(2,1)S(1)}, bf16[4,32,1024]{2,1,0:T(8,128)(2,1)S(1)}, u32[]{:S(2)}, u32[]{:S(2)}) collective-permute-start(bf16[4,32,1024]{2,1,0:T(8,128)(2,1)S(1)} %collective-permute-done.18.refs_4_), channel_id=1, source_target_pairs={{0,8},{8,0},{1,9},{9,1},{2,10},{10,2},{3,11},{11,3},{4,12},{12,4},... | collective-permute-start | bytes 786440 | tf_op jit(solution)/shard_map/ppermute | solution.py:40
  101.2 78.6 %reduce-scatter.5.cloned.1.call-start = ((), (), s32[]{:S(2)}) async-start(), calls=%async_computation.3 | async-start | bytes 995328 | tf_op jit(solution)/shard_map/reduce_scatter | solution.py:375
  104.7 16.0 %collective-permute-start.23 = (bf16[2,864,128]{2,1,0:T(8,128)(2,1)S(1)}, bf16[2,864,128]{2,1,0:T(8,128)(2,1)}, u32[]{:S(2)}, u32[]{:S(2)}) collective-permute-start(bf16[2,864,128]{2,1,0:T(8,128)(2,1)S(1)} %get-tuple-element.30), channel_id=1, source_target_pairs={{0,64},{64,0},{1,65},{65,1},{2,66},{66,2},{3,67},{67,3},{4,68},{68... | collective-permute-start | bytes 1327112 | tf_op jit(solution)/shard_map/ppermute | solution.py:40
  106.8 17.8 %collective-permute-start.22 = (bf16[864,128]{1,0:T(8,128)(2,1)S(1)}, bf16[864,128]{1,0:T(8,128)(2,1)S(1)}, u32[]{:S(2)}, u32[]{:S(2)}) collective-permute-start(bf16[864,128]{1,0:T(8,128)(2,1)S(1)} %get-tuple-element.29), channel_id=1, source_target_pairs={{0,8},{8,0},{1,9},{9,1},{2,10},{10,2},{3,11},{11,3},{4,12},{12,4},... | collective-permute-start | bytes 663560 | tf_op jit(solution)/shard_map/ppermute | solution.py:40
  133.9 8.8 %collective-permute-start.25 = (bf16[2,4,128,128]{3,2,1,0:T(8,128)(2,1)S(1)}, bf16[2,4,128,128]{3,2,1,0:T(8,128)(2,1)S(1)}, u32[]{:S(2)}, u32[]{:S(2)}) collective-permute-start(bf16[2,4,128,128]{3,2,1,0:T(8,128)(2,1)S(1)} %get-tuple-element.32), channel_id=1, source_target_pairs={{0,16},{16,32},{32,48},{48,0},{1,17},{17,33},{33,49},{49,1},{2,18}... | collective-permute-start | bytes 786440 | tf_op jit(solution)/shard_map/ppermute | solution.py:40
  134.9 14.6 %collective-permute-start.26 = (bf16[2,4,128,128]{3,2,1,0:T(8,128)(2,1)S(1)}, bf16[2,4,128,128]{3,2,1,0:T(8,128)(2,1)S(1)}, u32[]{:S(2)}, u32[]{:S(2)}) collective-permute-start(bf16[2,4,128,128]{3,2,1,0:T(8,128)(2,1)S(1)} %get-tuple-element.33), channel_id=1, source_target_pairs={{0,32},{16,48},{32,0},{48,16},{1,33},{17,49},{33,1},{49,17},{2,34}... | collective-permute-start | bytes 786440 | tf_op jit(solution)/shard_map/ppermute | solution.py:40
  137.8 11.7 %collective-permute-start.27 = (bf16[2,4,128,128]{3,2,1,0:T(8,128)(2,1)S(1)}, bf16[2,4,128,128]{3,2,1,0:T(8,128)(2,1)S(1)}, u32[]{:S(2)}, u32[]{:S(2)}) collective-permute-start(bf16[2,4,128,128]{3,2,1,0:T(8,128)(2,1)S(1)} %get-tuple-element.34), channel_id=1, source_target_pairs={{0,48},{16,0},{32,16},{48,32},{1,49},{17,1},{33,17},{49,33},{2,50}... | collective-permute-start | bytes 786440 | tf_op jit(solution)/shard_map/ppermute | solution.py:40
  149.7 8.0 %collective-permute-start.29 = (bf16[4,128,128]{2,1,0:T(8,128)(2,1)S(1)}, bf16[4,128,128]{2,1,0:T(8,128)(2,1)S(1)}, u32[]{:S(2)}, u32[]{:S(2)}) collective-permute-start(bf16[4,128,128]{2,1,0:T(8,128)(2,1)S(1)} %get-tuple-element.41), channel_id=1, source_target_pairs={{0,64},{64,0},{1,65},{65,1},{2,66},{66,2},{3,67},{67,3},{4,68},{68... | collective-permute-start | bytes 393224 | tf_op jit(solution)/shard_map/ppermute | solution.py:40
  153.3 40.3 %collective-permute-start.28 = (bf16[4,128,128]{2,1,0:T(8,128)(2,1)S(1)}, bf16[4,128,128]{2,1,0:T(8,128)(2,1)S(1)}, u32[]{:S(2)}, u32[]{:S(2)}) collective-permute-start(bf16[4,128,128]{2,1,0:T(8,128)(2,1)S(1)} %get-tuple-element.42.a), channel_id=1, source_target_pairs={{0,8},{8,0},{1,9},{9,1},{2,10},{10,2},{3,11},{11,3},{4,12},{12,4},... | collective-permute-start | bytes 393224 | tf_op jit(solution)/shard_map/ppermute | solution.py:40
  157.7 35.9 %collective-permute-start.30 = (bf16[4,128,128]{2,1,0:T(8,128)(2,1)S(1)}, bf16[4,128,128]{2,1,0:T(8,128)(2,1)S(1)}, u32[]{:S(2)}, u32[]{:S(2)}) collective-permute-start(bf16[4,128,128]{2,1,0:T(8,128)(2,1)S(1)} %collective-permute-done.29.c), channel_id=1, source_target_pairs={{0,8},{8,0},{1,9},{9,1},{2,10},{10,2},{3,11},{11,3},{4,12},{12,4},... | collective-permute-start | bytes 393224 | tf_op jit(solution)/shard_map/ppermute | solution.py:40
  180.8 5.3 %collective-permute-start.31 = (bf16[2,2,36,384]{3,2,0,1:T(8,128)(2,1)S(1)}, bf16[2,2,36,384]{3,2,0,1:T(8,128)(2,1)S(1)}, u32[]{:S(2)}, u32[]{:S(2)}) collective-permute-start(bf16[2,2,36,384]{3,2,0,1:T(8,128)(2,1)S(1)} %slice_bitcast_fusion.8), channel_id=1, source_target_pairs={{0,64},{64,0},{1,65},{65,1},{2,66},{66,2},{3,67},{67,3},{4,68},{68... | collective-permute-start | bytes 331784 | tf_op jit(solution)/shard_map/ppermute | solution.py:40
  186.2 9.5 %collective-permute-start.32 = (bf16[2,2,36,384]{3,2,0,1:T(8,128)(2,1)S(1)}, bf16[2,2,36,384]{3,2,0,1:T(8,128)(2,1)S(1)}, u32[]{:S(2)}, u32[]{:S(2)}) collective-permute-start(bf16[2,2,36,384]{3,2,0,1:T(8,128)(2,1)S(1)} %pad_maximum_fusion), channel_id=1, source_target_pairs={{0,8},{8,0},{1,9},{9,1},{2,10},{10,2},{3,11},{11,3},{4,12},{12,4},... | collective-permute-start | bytes 331784 | tf_op jit(solution)/shard_map/ppermute | solution.py:40
  (29 other events, 129.5 us)
Sparse Core Ops, SparseCore 0:
  10.2 26.2 all-gather.4
  56.3 22.5 all-gather.6
  101.3 38.7 reduce-scatter.2
  142.6 37.2 reduce-scatter.4
where the time goes:
time: 205 us; the launch traced here: 204 us
  waiting for transfers between devices  69.9 us (34%)
  starting transfers between devices  64.7 us (32%)
  Pallas kernels  38.2 us (19%)
  local copies, waits for them, and re-layouts  15.9 us (8%)
  between operations  14.1 us (7%)
    ppermute x29, starting transfers between devices, from_ahead(): return lax.ppermute(value, axis, [(i, (i - step) % n) for i in range(n)])  55.5 us
    ppermute x29, waiting for transfers between devices, from_ahead(): return lax.ppermute(value, axis, [(i, (i - step) % n) for i in range(n)])  35.1 us
    reduce_scatter x1, waiting for transfers between devices, body(): filter2_sum = lax.psum_scatter(filter2_parts, GZ, scatter_dimension=0)  20.1 us
    pallas_call x2, Pallas kernels, filter_sums(): pl.pallas_call(filter_kernel, out_shape=shape((8, SRC * TAPS * 4, 3 * WID...  16.9 us
    unnamed x53, local copies, waits for them, and re-layouts  11.8 us
    ppermute x2, waiting for transfers between devices, gather_grads(): high = lax.ppermute(own[:1], GZ, [(i + 1, i) for i in range(7)])  11.4 us
    pallas_call x1, Pallas kernels, data_by_row(): pl.pallas_call(data_by_row_kernel, out_shape=(shape((2, DEPTH, WIDE, WIDE...  8.09 us
    pallas_call x1, Pallas kernels, data_by_channel(): pl.pallas_call(data_by_channel_kernel, out_shape=(shape((DEPTH, BLOCK, CE...  6.92 us
  transfers between devices with their start and end apart: 37, of which 16 were waited for; matrix products, arithmetic and copies ran while one was open for 2% of the time, Pallas kernels for 18%

commit v1 on v0

v1 whole, which is shorter than its diff:
```python
import functools

import jax
import jax.numpy as jnp
from jax import lax
from jax.experimental import pallas as pl
from jax.experimental.pallas import tpu as pltpu
from jax.sharding import Mesh
from jax.sharding import PartitionSpec as P

AF = ("yh", "x", "core")
GZ = ("z", "yl")
SIZE = {"yh": 2, "x": 4, "core": 2, "z": 4, "yl": 2}
ROW = 32
CELLS = 1024
TAPS = 9
BLOCK = 32
WIDE = 128
DEPTH = 4
SRC = 4
DEEP = TAPS * BLOCK
K = SRC * DEEP
VMEM_BYTES = 20 * 1024 * 1024
NN = (((1,), (0,)), ((), ()))
NT = (((1,), (1,)), ((), ()))
COST = pl.CostEstimate(flops=1000, bytes_accessed=1000, transcendentals=0)
F32 = jnp.float32
BF16 = jnp.bfloat16


def params():
    return pltpu.CompilerParams(vmem_limit_bytes=VMEM_BYTES)


def whole(count):
    return [pl.BlockSpec(memory_space=pltpu.VMEM)] * count


def from_ahead(value, axis, step):
    n = SIZE[axis]
    return lax.ppermute(value, axis, [(i, (i - step) % n) for i in range(n)])


def shape(dims, kind=BF16):
    return jax.ShapeDtypeStruct(dims, kind)


def picks(place_ref, dyh, dcore):
    yh, x, core = place_ref[0], place_ref[1], place_ref[2]
    row = lax.broadcasted_iota(jnp.int32, (WIDE, 512), 0)
    lane = lax.broadcasted_iota(jnp.int32, (WIDE, 512), 1)
    column = (row // BLOCK + x) % 4
    channel = (yh + dyh) % 2 * 256 + (core + dcore) % 2 * BLOCK + column * 64 + row % BLOCK
    return jnp.where(channel == lane, 1.0, 0.0).astype(BF16)


def orders_kernel(place_ref, out_ref):
    for src in range(SRC):
        out_ref[src * WIDE : (src + 1) * WIDE, :] = picks(place_ref, src // 2, src % 2)


def make_orders(place):
    return pl.pallas_call(
        orders_kernel,
        out_shape=shape((512, 512)),
        in_specs=[pl.BlockSpec(memory_space=pltpu.SMEM)],
        out_specs=whole(1)[0],
        compiler_params=params(),
        cost_estimate=COST,
        name="orders",
    )(place)


def regroup_kernel(w_ref, order_ref, own_ref, core_ref, far_ref):
    rows = w_ref[...]
    for block, target in enumerate((own_ref, core_ref, far_ref.at[0], far_ref.at[1])):
        order = order_ref[block * WIDE : (block + 1) * WIDE, :]
        picked = lax.dot_general(rows, order, NT, preferred_element_type=F32)
        target[...] = picked.astype(BF16)


def regroup(weight, order):
    rows = weight.reshape(27 * BLOCK, 512)
    one = shape((27 * BLOCK, WIDE))
    return pl.pallas_call(
        regroup_kernel,
        out_shape=(one, one, shape((2, 27 * BLOCK, WIDE))),
        in_specs=whole(2),
        out_specs=tuple(whole(3)),
        compiler_params=params(),
        cost_estimate=COST,
        name="regroup",
    )(rows, order)


def masks():
    lane = lax.broadcasted_iota(jnp.int32, (BLOCK, CELLS), 1)
    col = lane & (ROW - 1)
    one = lambda keep: jnp.where(keep, 1.0, 0.0).astype(BF16)
    return (
        one(col < ROW - 1),
        one(col > 0),
        one(lane < CELLS - ROW),
        one(lane >= ROW),
    )


def shift_plane(refs, shifted, keep):
    left, right, top, bottom = keep
    for src, ref in enumerate(refs):
        mid = ref[...]
        across = (
            pltpu.roll(mid, CELLS - 1, 1) * left,
            mid,
            pltpu.roll(mid, 1, 1) * right,
        )
        for kx in range(3):
            rows = (
                pltpu.roll(across[kx], CELLS - ROW, 1) * top,
                across[kx],
                pltpu.roll(across[kx], ROW, 1) * bottom,
            )
            for ky in range(3):
                at = src * DEEP + (ky * 3 + kx) * BLOCK
                shifted[at : at + BLOCK, :] = rows[ky]


def four(own, far, got):
    return own, got.at[0], far, got.at[1]


def plane_refs(grads, plane):
    at = {0: DEPTH, DEPTH + 1: DEPTH + 1}.get(plane, plane - 1)
    return [ref.at[at] for ref in four(*grads)]


def taps_of(plane):
    return max(0, 2 - plane), min(3, DEPTH + 2 - plane)


def data_sums(grads, weights, turned, shifted, total):
    own, far, got = weights
    for kz in range(3):
        rows = slice(kz * DEEP, (kz + 1) * DEEP)
        for src, block in enumerate((own[rows], got[0, rows], far[0, rows], got[1, rows])):
            shifted[0, src * DEEP : (src + 1) * DEEP, :WIDE] = block
        turned[kz * WIDE : (kz + 1) * WIDE, :] = shifted[0, :, :WIDE].T
    keep = masks()
    for plane in range(DEPTH + 2):
        slot = shifted.at[plane % 2]
        shift_plane(plane_refs(grads, plane), slot, keep)
        low, high = taps_of(plane)
        for part in range(4):
            lanes = slice(part * 256, (part + 1) * 256)
            part = lax.dot_general(
                turned[low * WIDE : high * WIDE, :], slot[:, lanes], NN, preferred_element_type=F32
            )
            for kz in range(low, high):
                at = (plane - 2 + kz) * WIDE
                piece = part[(kz - low) * WIDE : (kz - low + 1) * WIDE]
                if kz < 2:
                    piece = piece + total[at : at + WIDE, lanes]
                total[at : at + WIDE, lanes] = piece


def data_by_channel_kernel(*refs):
    grads, weights, outs = refs[:3], refs[3:6], refs[6:10]
    total = refs[-1]
    data_sums(grads, weights, *refs[10:])
    for dx in range(4):

        @pl.loop(0, DEPTH)
        def _(plane):
            at = pl.multiple_of(plane * WIDE + dx * BLOCK, BLOCK)
            outs[dx][plane] = total[pl.ds(at, BLOCK), :].astype(BF16)


def data_by_row_kernel(place_ref, *refs):
    grads, weights, outs = refs[:3], refs[3:6], refs[6:10]
    total = refs[-1]
    data_sums(grads, weights, *refs[10:])
    yh, x = place_ref[0], place_ref[1]
    for dx in range(4):

        @pl.loop(0, 2 * DEPTH)
        def _(step):
            dyh, plane = step // DEPTH, step % DEPTH
            chunk = (yh + dyh) % 2 * 4 + (x + dx) % 4
            lanes = pl.ds(pl.multiple_of(chunk * WIDE, WIDE), WIDE)
            for block in range(4):
                at = pl.multiple_of(plane * WIDE + (dx + block) % 4 * BLOCK, BLOCK)
                outs[dx][dyh, plane, block * BLOCK : (block + 1) * BLOCK] = total[pl.ds(at, BLOCK), lanes].astype(BF16)


DATA_SCRATCH = [
    pltpu.VMEM((3 * WIDE, K), BF16),
    pltpu.VMEM((2, K, CELLS), BF16),
    pltpu.VMEM((DEPTH * WIDE, CELLS), F32),
]


def data_by_channel(grads, weights):
    return pl.pallas_call(
        data_by_channel_kernel,
        out_shape=(shape((DEPTH, BLOCK, CELLS)),) * 4,
        in_specs=whole(6),
        out_specs=tuple(whole(4)),
        scratch_shapes=DATA_SCRATCH,
        compiler_params=params(),
        cost_estimate=COST,
        name="data_by_channel",
    )(*grads, *weights)


def data_by_row(place, grads, weights):
    return pl.pallas_call(
        data_by_row_kernel,
        out_shape=(shape((2, DEPTH, WIDE, WIDE)),) * 4,
        in_specs=[pl.BlockSpec(memory_space=pltpu.SMEM)] + whole(6),
        out_specs=tuple(whole(4)),
        scratch_shapes=DATA_SCRATCH,
        compiler_params=params(),
        cost_estimate=COST,
        name="data_by_row",
    )(place, *grads, *weights)


def add_products(total, slot, sources, low, high, fresh):
    for src in range(SRC):
        part = lax.dot_general(
            slot[src * DEEP : (src + 1) * DEEP, :], sources, NT, preferred_element_type=F32
        )
        for kz in range(low, high):
            piece = part[:, (kz - low) * WIDE : (kz - low + 1) * WIDE]
            lanes = slice(kz * WIDE, (kz + 1) * WIDE)
            piece = piece.reshape(TAPS, 4, 8, WIDE)
            rows = slice(src * TAPS, (src + 1) * TAPS)
            if not fresh(kz):
                piece = piece + total[rows, :, :, lanes]
            total[rows, :, :, lanes] = piece


def filter_total(grads, sources, first_plane, stacked, shifted, total):
    for dx in range(4):
        for plane in range(DEPTH):
            at = plane * WIDE + dx * BLOCK
            stacked[at : at + BLOCK, :] = sources[dx][first_plane + plane]
    keep = masks()
    for plane in range(DEPTH + 2):
        slot = shifted.at[plane % 2]
        shift_plane(plane_refs(grads, plane), slot, keep)
        low, high = taps_of(plane)
        first = plane - 2 + low
        rows = stacked[first * WIDE : (first + high - low) * WIDE, :]
        add_products(total, slot, rows, low, high, lambda kz: plane == 2 - kz)


def second_filter_kernel(place_ref, *refs):
    filter_total(refs[:3], refs[3:7], 0, *refs[8:])
    for z in range(4):
        low, high = rows_of(refs[-1], z)
        refs[7][z, 0], refs[7][z, 1] = low, high


def first_filter_kernel(place_ref, *refs):
    filter_total(refs[:3], refs[3:7], DEPTH, *refs[11:])
    for dz in range(4):
        low, high = rows_of(refs[-1], (place_ref[3] + dz) % 4)
        refs[7 + dz][0], refs[7 + dz][1] = low, high


def rows_of(total, z):
    upper = lax.broadcasted_iota(jnp.int32, (18, 8, 3 * WIDE), 1) < 4
    rows = total[:, pl.ds(z, 1), :, :].reshape(18, 2, 8, 3 * WIDE)
    one, two = rows[:, 0], rows[:, 1]
    low = jnp.where(upper, one, pltpu.roll(two, 4, 1))
    high = jnp.where(upper, pltpu.roll(one, 4, 1), two)
    return [half.reshape(18 * 8, 3 * WIDE).astype(BF16) for half in (low, high)]


def filter_sums(kernel, out_shape, *args):
    return pl.pallas_call(
        kernel,
        out_shape=out_shape,
        in_specs=[pl.BlockSpec(memory_space=pltpu.SMEM)] + whole(len(args) - 1),
        out_specs=jax.tree.map(lambda _: whole(1)[0], out_shape),
        scratch_shapes=[
            pltpu.VMEM((DEPTH * WIDE, CELLS), BF16),
            pltpu.VMEM((2, K, CELLS), BF16),
            pltpu.VMEM((SRC * TAPS, 4, 8, 3 * WIDE), F32),
        ],
        compiler_params=params(),
        cost_estimate=COST,
        name="filter_sums",
    )(*args)


def both_cores(near, far):
    return from_ahead(jnp.stack([near, far]), "core", 1)


def moved_ahead(blocks, axis):
    return [blocks[0]] + [from_ahead(blocks[d], axis, -d) for d in range(1, 4)]


def total_of(blocks):
    return sum(block.astype(F32) for block in blocks)


def halo(last, first):
    low = lax.ppermute(last, GZ, [(i, i + 1) for i in range(7)])
    high = lax.ppermute(first, GZ, [(i + 1, i) for i in range(7)])
    return low, high


def sum_yl(part):
    yl = lax.axis_index("yl")
    mine = lax.dynamic_index_in_dim(part, yl, 0, keepdims=False)
    other = lax.dynamic_index_in_dim(part, 1 - yl, 0, keepdims=False)
    return total_of([mine, from_ahead(other, "yl", 1)]).astype(BF16)


def place_filters_kernel(factor_ref, order_ref, own_ref, far_ref, got_ref, first_ref, second_ref):
    orders = [order_ref[src * WIDE : (src + 1) * WIDE, :] for src in range(SRC)]
    for index, out_ref in enumerate((first_ref, second_ref)):
        for kz in range(3):
            lanes = slice(kz * WIDE, (kz + 1) * WIDE)
            total = None
            for order, rows in zip(
                orders,
                (own_ref[index, :, lanes], got_ref[0, index, :, lanes], far_ref[index, :, lanes], got_ref[1, index, :, lanes]),
            ):
                part = lax.dot_general(rows, order, NN, preferred_element_type=F32)
                total = part if total is None else total + part
            total = total * factor_ref[0]
            for tap in range(TAPS):
                out_ref[kz * TAPS + tap] = total[tap * 4 : (tap + 1) * 4]


def finish_filters(order, sums, factor):
    rows = sums.reshape(2, 2, 2, TAPS * 4, 3 * WIDE).transpose(1, 2, 0, 3, 4)
    far = from_ahead(rows[1], "yh", 1)
    got = both_cores(rows[0, 1], far[1])
    outs = pl.pallas_call(
        place_filters_kernel,
        out_shape=(shape((27, 4, 512), F32),) * 2,
        in_specs=[pl.BlockSpec(memory_space=pltpu.SMEM)] + whole(4),
        out_specs=tuple(whole(2)),
        compiler_params=params(),
        cost_estimate=COST,
        name="place_filters",
    )(factor.reshape(1), order, rows[0, 0], far[0], got)
    return [out.reshape(3, 3, 3, 4, 512) for out in outs]


def place_kernel(place_ref, order_ref, own_ref, far_ref, got_ref, out_ref):
    upper = place_ref[2] == 1
    for pair in range(DEPTH // 2):
        halves = []
        for plane in (2 * pair, 2 * pair + 1):
            rows = jnp.concatenate([ref[plane] for ref in four(own_ref, far_ref, got_ref)], axis=0)
            halves.append(jnp.where(upper, rows[:, 64:], rows[:, :64]))
        cells = jnp.concatenate(halves, axis=1).T
        part = lax.dot_general(cells, order_ref[...], NN, preferred_element_type=F32).astype(BF16)
        out_ref[2 * pair], out_ref[2 * pair + 1] = part[:64], part[64:]


def finish_image(part, place, order):
    near = part[0]
    far = from_ahead(part[1], "yh", 1)
    out = pl.pallas_call(
        place_kernel,
        out_shape=shape((DEPTH, 64, 512)),
        in_specs=[pl.BlockSpec(memory_space=pltpu.SMEM)] + whole(4),
        out_specs=whole(1)[0],
        compiler_params=params(),
        cost_estimate=COST,
        name="place",
    )(place, order, near, far, both_cores(near, far))
    return out.reshape(DEPTH, 2, ROW, 512)


def after(value, *done):
    return lax.optimization_barrier((value,) + done)[0]


def body(inputs, preact, cotangent, weight1, weight2):
    place = jnp.stack([lax.axis_index(a) for a in AF + ("z",)]).astype(jnp.int32)
    factor = 1.0 / jnp.sqrt(F32(32 * CELLS))
    planes_first = lambda value: value.transpose(1, 0, 2)
    zero = jnp.zeros((), BF16)
    gather_inputs = lambda value: [value] + [from_ahead(value, "x", d) for d in (1, 2, 3)]

    order = make_orders(place)
    cot = planes_first(cotangent)
    far_cot = from_ahead(cot, "yh", 1)
    low, high = halo(cot[DEPTH - 1 :], cot[:1])
    rims = jnp.concatenate([low, high])
    pre = planes_first(preact)
    sources = gather_inputs(jnp.concatenate([jnp.maximum(pre, zero), planes_first(inputs)]))
    own2, core2, far2 = regroup(weight2, order)
    far2 = from_ahead(after(far2, low, high, far_cot), "yh", 1)
    far_rims = from_ahead(rims, "yh", 1)
    cot, far_cot = jnp.concatenate([cot, rims]), jnp.concatenate([far_cot, far_rims])
    grads2 = cot, far_cot, both_cores(cot, far_cot)
    weights2 = own2, far2, both_cores(core2, far2[1])
    own1, core1, far1 = regroup(weight1, after(order, low))

    unit_parts = data_by_channel(grads2, after(weights2, own1))
    far1 = from_ahead(after(far1, unit_parts[0]), "yh", 1)
    whole_filter = shape((4, 2, SRC * TAPS * 4, 3 * WIDE))
    filter2_parts = filter_sums(
        second_filter_kernel, whole_filter, after(place, unit_parts[0]), *grads2, *sources
    )
    blocks = after(moved_ahead(unit_parts, "x"), filter2_parts)
    grad = jnp.where(pre > 0, total_of(blocks), 0.0).astype(BF16)
    grad = after(grad, far1)
    far_grad = from_ahead(grad, "yh", 1)
    low, high = halo(grad[DEPTH - 1 :], grad[:1])
    rims = jnp.concatenate([low, high])
    far_rims = from_ahead(rims, "yh", 1)
    filter2_got = lax.all_to_all(after(filter2_parts, far_grad), "z", 0, 0)
    weights1 = own1, far1, both_cores(after(core1, low), far1[1])
    grad, far_grad = jnp.concatenate([grad, rims]), jnp.concatenate([far_grad, far_rims])
    grads1 = grad, far_grad, both_cores(grad, far_grad)
    filter1_parts = filter_sums(
        first_filter_kernel, (shape(whole_filter.shape[1:]),) * 4, place, *grads1, *sources
    )
    image_parts = data_by_row(after(place, filter1_parts), grads1, weights1)
    filter1_got = after(moved_ahead(filter1_parts, "z"), image_parts[0])
    sums = [total_of(list(got)).astype(BF16) for got in (filter1_got, filter2_got)]
    sums = sum_yl(jnp.stack(sums, axis=1))
    blocks = after(moved_ahead(image_parts, "x"), sums)
    input_grad = finish_image(total_of(blocks).astype(BF16), place, order)
    filter1_grad, filter2_grad = finish_filters(order, sums, factor)
    return input_grad, filter1_grad, filter2_grad


def solution(mesh):
    fine = Mesh(mesh.devices.reshape(2, 4, 2, 4, 2), AF + GZ)
    placed = (
        P(AF, GZ, None),
        P(AF, GZ, None),
        P(AF, GZ, None),
        P(None, None, None, AF, None),
        P(None, None, None, AF, None),
    )
    return jax.shard_map(
        body,
        mesh=fine,
        in_specs=placed,
        out_specs=(
            P(GZ, AF, None, None),
            P(None, None, None, AF + GZ, None),
            P(None, None, None, AF + GZ, None),
        ),
        check_vma=False,
    )
```

time: 205 us -> 155 us (0.76)
  waiting for transfers between devices: 69.9 us -> 39.8 us
  between operations: 14.1 us -> 1.11 us
  local copies, waits for them, and re-layouts: 15.9 us -> 6.07 us
  other arithmetic: 1.31 us -> 6.74 us
  starting transfers between devices: 64.7 us -> 62.6 us
    reduce_scatter x2 -> x0, waiting for transfers between devices: 20.1 us -> none  [the longest x1 20.1 us: body(): filter2_sum = lax.psum_scatter(filter2_parts, GZ, scatter_dimension=0)]
    unnamed x53 -> x41, local copies, waits for them, and re-layouts: 11.8 us -> 4.79 us
    ppermute x4, waiting for transfers between devices: 14.8 us -> 8.29 us  [the longest x2 6.21 us: halo(): high = lax.ppermute(first, GZ, [(i + 1, i) for i in range(7)])]
    ppermute x29 -> x27, starting transfers between devices: 55.5 us -> 50.2 us  [from_ahead(): return lax.ppermute(value, axis, [(i, (i - step) % n) for i in range(n)])]
    all_to_all x0 -> x1, starting transfers between devices: none -> 4.57 us  [body(): filter2_got = lax.all_to_all(after(filter2_parts, far_grad), 'z', 0, 0)]
    ppermute x29 -> x27, waiting for transfers between devices: 35.1 us -> 31.5 us  [from_ahead(): return lax.ppermute(value, axis, [(i, (i - step) % n) for i in range(n)])]
    another operation x2 -> x9, other arithmetic: 0.1 us -> 3.59 us  [the longest x7 2.01 us: both_cores(): return from_ahead(jnp.stack([near, far]), 'core', 1)]
    pallas_call x3 -> x4, Pallas kernels: 17.8 us -> 18.4 us  [the longest x2 16.4 us: filter_sums(): pl.pallas_call(kernel, out_shape=out_shape, in_specs=[pl.BlockSpec(memory...]
  transfers between devices with their start and end apart: 37 -> 32, of which waited for: 16 -> 15; matrix products, arithmetic and copies ran while one was open for 2% -> 3% of each run, Pallas kernels for 18% -> 23%
where the time goes in v1:
time: 155 us; the launch traced here: 154 us
  starting transfers between devices  62.6 us (40%)
  waiting for transfers between devices  39.8 us (26%)
  Pallas kernels  37.9 us (24%)
  other arithmetic  6.74 us (4%)
  local copies, waits for them, and re-layouts  6.07 us (4%)
    ppermute x27, starting transfers between devices, from_ahead(): return lax.ppermute(value, axis, [(i, (i - step) % n) for i in range(n)])  50.2 us
    ppermute x27, waiting for transfers between devices, from_ahead(): return lax.ppermute(value, axis, [(i, (i - step) % n) for i in range(n)])  31.5 us
    pallas_call x2, Pallas kernels, filter_sums(): pl.pallas_call(kernel, out_shape=out_shape, in_specs=[pl.BlockSpec(memory...  16.4 us
    pallas_call x1, Pallas kernels, data_by_row(): pl.pallas_call(data_by_row_kernel, out_shape=(shape((2, DEPTH, WIDE, WIDE...  8.61 us
    pallas_call x1, Pallas kernels, data_by_channel(): pl.pallas_call(data_by_channel_kernel, out_shape=(shape((DEPTH, BLOCK, CE...  6.87 us
    ppermute x2, waiting for transfers between devices, halo(): high = lax.ppermute(first, GZ, [(i + 1, i) for i in range(7)])  6.21 us
    ppermute x2, starting transfers between devices, halo(): low = lax.ppermute(last, GZ, [(i, i + 1) for i in range(7)])  5.25 us
    unnamed x41, local copies, waits for them, and re-layouts  4.79 us
  transfers between devices with their start and end apart: 32, of which 15 were waited for; matrix products, arithmetic and copies ran while one was open for 3% of the time, Pallas kernels for 23%

profile of v1, /device:TPU:1, one launch (start us, length us, event | category | flops | bytes accessed | tf_op | source)
XLA Modules:
  0.0 154.2 jit_solution(4934344156808121909)
XLA Ops:
  1.8 3.8 %collective-permute-start.2 = (bf16[4,32,1024]{2,1,0:T(8,128)(2,1)S(1)}, bf16[4,32,1024]{2,1,0:T(8,128)(2,1)S(1)}, u32[]{:S(2)}, u32[]{:S(2)}) collective-permute-start(bf16[4,32,1024]{2,1,0:T(8,128)(2,1)S(1)} %bitcast.61), channel_id=1, source_target_pairs={{0,64},{64,0},{1,65},{65,1},{2,66},{66,2},{3,67},{67,3},{4,68},{68... | collective-permute-start | bytes 786440 | tf_op jit(solution)/shard_map/ppermute | solution.py:41
  5.6 2.3 %collective-permute-start = (bf16[1,32,1024]{2,1,0:T(8,128)(2,1)S(1)}, bf16[1,32,1024]{2,1,0:T(8,128)(2,1)S(1)}, u32[]{:S(2)}, u32[]{:S(2)}) collective-permute-start(bf16[1,32,1024]{2,1,0:T(8,128)(2,1)S(1)} %get-tuple-element.96), channel_id=1, source_target_pairs={{0,1},{1,2},{2,3},{3,4},{4,5},{5,6},{6,7},{8,9},{9,10},{10,11},{11... | collective-permute-start | bytes 196616 | tf_op jit(solution)/shard_map/ppermute | solution.py:311
  12.0 2.7 %collective-permute-done.1 = bf16[1,32,1024]{2,1,0:T(8,128)(2,1)S(1)} collective-permute-done((bf16[1,32,1024]{2,1,0:T(8,128)(2,1)S(1)}, bf16[1,32,1024]{2,1,0:T(8,128)(2,1)S(1)}, u32[]{:S(2)}, u32[]{:S(2)}) %collective-permute-start.1) | collective-permute-done | bytes 65568 | tf_op jit(solution)/shard_map/ppermute | solution.py:312
  17.9 2.2 %collective-permute-done.3 = bf16[2,32,1024]{2,1,0:T(8,128)(2,1)S(1)} collective-permute-done((bf16[2,32,1024]{2,1,0:T(8,128)(2,1)S(1)}, bf16[2,32,1024]{2,1,0:T(8,128)(2,1)S(1)}, u32[]{:S(2)}, u32[]{:S(2)}) %collective-permute-start.3) | collective-permute-done | bytes 131104 | tf_op jit(solution)/shard_map/ppermute | solution.py:41
  20.2 4.0 %collective-permute-start.4 = (bf16[2,6,32,1024]{3,2,1,0:T(8,128)(2,1)S(1)}, bf16[2,6,32,1024]{3,2,1,0:T(8,128)(2,1)S(1)}, u32[]{:S(2)}, u32[]{:S(2)}) collective-permute-start(bf16[2,6,32,1024]{3,2,1,0:T(8,128)(2,1)S(1)} %pad_maximum_fusion), channel_id=1, source_target_pairs={{0,8},{8,0},{1,9},{9,1},{2,10},{10,2},{3,11},{11,3},{4,12},{12,4},... | collective-permute-start | bytes 2359304 | tf_op jit(solution)/shard_map/ppermute | solution.py:41
  24.6 2.5 %collective-permute-start.10 = (bf16[8,32,1024]{2,1,0:T(8,128)(2,1)S(1)}, bf16[8,32,1024]{2,1,0:T(8,128)(2,1)S(1)}, u32[]{:S(2)}, u32[]{:S(2)}) collective-permute-start(bf16[8,32,1024]{2,1,0:T(8,128)(2,1)S(1)} %pad_maximum_fusion.2.refs_3_), channel_id=1, source_target_pairs={{0,48},{16,0},{32,16},{48,32},{1,49},{17,1},{33,17},{49,33},{2,50}... | collective-permute-start | bytes 1572872 | tf_op jit(solution)/shard_map/ppermute | solution.py:41
  27.2 2.5 %collective-permute-done.5.refs_4_ = bf16[2,864,128]{2,1,0:T(8,128)(2,1)S(1)} collective-permute-done((bf16[2,864,128]{2,1,0:T(8,128)(2,1)S(1)}, bf16[2,864,128]{2,1,0:T(8,128)(2,1)S(1)}, u32[]{:S(2)}, u32[]{:S(2)}) %collective-permute-start.5) | collective-permute-done | bytes 442400 | tf_op jit(solution)/shard_map/ppermute | solution.py:41
  29.8 2.2 %collective-permute-start.6 = (bf16[2,864,128]{2,1,0:T(8,128)(2,1)S(1)}, bf16[2,864,128]{2,1,0:T(8,128)(2,1)S(1)}, u32[]{:S(2)}, u32[]{:S(2)}) collective-permute-start(bf16[2,864,128]{2,1,0:T(8,128)(2,1)S(1)} %pad_maximum_fusion.3), channel_id=1, source_target_pairs={{0,8},{8,0},{1,9},{9,1},{2,10},{10,2},{3,11},{11,3},{4,12},{12,4},... | collective-permute-start | bytes 1327112 | tf_op jit(solution)/shard_map/ppermute | solution.py:41
  31.9 2.8 %collective-permute-start.11 = (bf16[8,32,1024]{2,1,0:T(8,128)(2,1)S(1)}, bf16[8,32,1024]{2,1,0:T(8,128)(2,1)S(1)}, u32[]{:S(2)}, u32[]{:S(2)}) collective-permute-start(bf16[8,32,1024]{2,1,0:T(8,128)(2,1)S(1)} %pad_maximum_fusion.2.refs_3_), channel_id=1, source_target_pairs={{0,32},{16,48},{32,0},{48,16},{1,33},{17,49},{33,1},{49,17},{2,34}... | collective-permute-start | bytes 1572872 | tf_op jit(solution)/shard_map/ppermute | solution.py:41
  37.5 6.9 %data_by_channel.1 = (bf16[4,32,1024]{2,1,0:T(8,128)(2,1)S(1)}, bf16[4,32,1024]{2,1,0:T(8,128)(2,1)S(1)}, bf16[4,32,1024]{2,1,0:T(8,128)(2,1)S(1)}, bf16[4,32,1024]{2,1,0:T(8,128)(2,1)S(1)}) custom-call(bf16[6,32,1024]{2,1,0:T(8,128)(2,1)S(1)} %get-tuple-element.90.refs_0_, bf16[6,32,1024]{2,1,0:T(8,128)(2,1)S(1)} %constant_dynamic-update-slice_fusion.refs_1_, ...), custom_call_target="tpu_custom_call" | custom-call | flops 1000 | bytes 1000 | tf_op jit(solution)/shard_map/data_by_channel/pallas_call | solution.py:203
  44.4 3.5 %collective-permute-start.8 = (bf16[4,32,1024]{2,1,0:T(8,128)(2,1)S(1)}, bf16[4,32,1024]{2,1,0:T(8,128)(2,1)S(1)}, u32[]{:S(2)}, u32[]{:S(2)}) collective-permute-start(bf16[4,32,1024]{2,1,0:T(8,128)(2,1)S(1)} %get-tuple-element.57), channel_id=1, source_target_pairs={{0,32},{16,48},{32,0},{48,16},{1,33},{17,49},{33,1},{49,17},{2,34}... | collective-permute-start | bytes 786440 | tf_op jit(solution)/shard_map/ppermute | solution.py:41
  49.8 8.8 %collective-permute-done.12.refs_6_ = bf16[8,32,1024]{2,1,0:T(8,128)(2,1)S(1)} collective-permute-done((bf16[8,32,1024]{2,1,0:T(8,128)(2,1)S(1)}, bf16[8,32,1024]{2,1,0:T(8,128)(2,1)S(1)}, u32[]{:S(2)}, u32[]{:S(2)}) %collective-permute-start.12) | collective-permute-done | bytes 524320 | tf_op jit(solution)/shard_map/ppermute | solution.py:41
  58.6 8.2 %filter_sums.2 = bf16[4,2,144,384]{3,2,1,0:T(8,128)(2,1)} custom-call(s32[4]{0:T(128)S(1)} %pad_add_fusion.place_ref, bf16[6,32,1024]{2,1,0:T(8,128)(2,1)S(1)} %get-tuple-element.90.refs_0_, bf16[6,32,1024]{2,1,0:T(8,128)(2,1)S(1)} %constant_dynamic-update-slice_fusion.refs_1_, bf16[2,6,32,1024]{3,2,1,0:T(8,128)(2,1)S(1)} %collective-permute-done.4.refs_2_, ...), custom_call_target="tpu_custom_call" | custom-call | flops 1000 | bytes 1000 | tf_op jit(solution)/shard_map/filter_sums/pallas_call | solution.py:282
  66.8 2.7 %collective-permute-done.8 = bf16[4,32,1024]{2,1,0:T(8,128)(2,1)S(1)} collective-permute-done((bf16[4,32,1024]{2,1,0:T(8,128)(2,1)S(1)}, bf16[4,32,1024]{2,1,0:T(8,128)(2,1)S(1)}, u32[]{:S(2)}, u32[]{:S(2)}) %collective-permute-start.8) | collective-permute-done | bytes 262176 | tf_op jit(solution)/shard_map/ppermute | solution.py:41
  71.4 2.9 %collective-permute-start.14 = (bf16[1,32,1024]{2,1,0:T(8,128)(2,1)S(1)}, bf16[1,32,1024]{2,1,0:T(8,128)(2,1)S(1)}, u32[]{:S(2)}, u32[]{:S(2)}) collective-permute-start(bf16[1,32,1024]{2,1,0:T(8,128)(2,1)S(1)} %get-tuple-element.95), channel_id=1, source_target_pairs={{0,1},{1,2},{2,3},{3,4},{4,5},{5,6},{6,7},{8,9},{9,10},{10,11},{11... | collective-permute-start | bytes 196616 | tf_op jit(solution)/shard_map/ppermute | solution.py:311
  76.9 3.5 %collective-permute-done.15 = bf16[1,32,1024]{2,1,0:T(8,128)(2,1)S(1)} collective-permute-done((bf16[1,32,1024]{2,1,0:T(8,128)(2,1)S(1)}, bf16[1,32,1024]{2,1,0:T(8,128)(2,1)S(1)}, u32[]{:S(2)}, u32[]{:S(2)}) %collective-permute-start.15) | collective-permute-done | bytes 65568 | tf_op jit(solution)/shard_map/ppermute | solution.py:312
  80.5 2.9 %collective-permute-start.17 = (bf16[2,32,1024]{2,1,0:T(8,128)(2,1)S(1)}, bf16[2,32,1024]{2,1,0:T(8,128)(2,1)S(1)}, u32[]{:S(2)}, u32[]{:S(2)}) collective-permute-start(bf16[2,32,1024]{2,1,0:T(8,128)(2,1)S(1)} %pad_maximum_fusion.8), channel_id=1, source_target_pairs={{0,64},{64,0},{1,65},{65,1},{2,66},{66,2},{3,67},{67,3},{4,68},{68... | collective-permute-start | bytes 393224 | tf_op jit(solution)/shard_map/ppermute | solution.py:41
  83.4 2.4 %collective-permute-done.17 = bf16[2,32,1024]{2,1,0:T(8,128)(2,1)S(1)} collective-permute-done((bf16[2,32,1024]{2,1,0:T(8,128)(2,1)S(1)}, bf16[2,32,1024]{2,1,0:T(8,128)(2,1)S(1)}, u32[]{:S(2)}, u32[]{:S(2)}) %collective-permute-start.17) | collective-permute-done | bytes 131104 | tf_op jit(solution)/shard_map/ppermute | solution.py:41
  86.8 4.8 %collective-permute-start.18 = (bf16[2,6,32,1024]{3,2,1,0:T(8,128)(2,1)}, bf16[2,6,32,1024]{3,2,1,0:T(8,128)(2,1)S(1)}, u32[]{:S(2)}, u32[]{:S(2)}) collective-permute-start(bf16[2,6,32,1024]{3,2,1,0:T(8,128)(2,1)} %pad_maximum_fusion.1), channel_id=1, source_target_pairs={{0,8},{8,0},{1,9},{9,1},{2,10},{10,2},{3,11},{11,3},{4,12},{12,4},... | collective-permute-start | bytes 2359304 | tf_op jit(solution)/shard_map/ppermute | solution.py:41
  91.6 4.6 %all-to-all-start = ((bf16[4,2,144,384]{3,2,1,0:T(8,128)(2,1)}), bf16[4,2,144,384]{3,2,1,0:T(8,128)(2,1)}, u32[]{:S(2)}, u32[]{:S(2)}) async-start(bf16[4,2,144,384]{3,2,1,0:T(8,128)(2,1)} %filter_sums.2), calls=%async_computation | async-start | bytes 1769472 | tf_op jit(solution)/shard_map/all_to_all | solution.py:422
  100.5 8.2 %filter_sums.3 = (bf16[2,144,384]{2,1,0:T(8,128)(2,1)S(1)}, bf16[2,144,384]{2,1,0:T(8,128)(2,1)}, bf16[2,144,384]{2,1,0:T(8,128)(2,1)}, bf16[2,144,384]{2,1,0:T(8,128)(2,1)}) custom-call(s32[4]{0:T(128)S(1)} %pad_add_fusion.place_ref, bf16[6,32,1024]{2,1,0:T(8,128)(2,1)S(1)} %constant_dynamic-update-slice_fusion.2.refs_0_, ...), custom_call_target="tpu_custom_call" | custom-call | flops 1000 | bytes 1000 | tf_op jit(solution)/shard_map/filter_sums/pallas_call | solution.py:282
  108.6 1.7 %collective-permute-start.23 = (bf16[2,144,384]{2,1,0:T(8,128)(2,1)}, bf16[2,144,384]{2,1,0:T(8,128)(2,1)}, u32[]{:S(2)}, u32[]{:S(2)}) collective-permute-start(bf16[2,144,384]{2,1,0:T(8,128)(2,1)} %get-tuple-element.68), channel_id=1, source_target_pairs={{0,2},{2,4},{4,6},{6,0},{1,3},{3,5},{5,7},{7,1},{8,10},{10,12},{12... | collective-permute-start | bytes 663560 | tf_op jit(solution)/shard_map/ppermute | solution.py:41
  110.4 2.4 %collective-permute-start.24 = (bf16[2,144,384]{2,1,0:T(8,128)(2,1)}, bf16[2,144,384]{2,1,0:T(8,128)(2,1)}, u32[]{:S(2)}, u32[]{:S(2)}) collective-permute-start(bf16[2,144,384]{2,1,0:T(8,128)(2,1)} %get-tuple-element.69), channel_id=1, source_target_pairs={{0,4},{2,6},{4,0},{6,2},{1,5},{3,7},{5,1},{7,3},{8,12},{10,14},{12... | collective-permute-start | bytes 663560 | tf_op jit(solution)/shard_map/ppermute | solution.py:41
  115.4 8.6 %data_by_row.1 = (bf16[2,4,128,128]{3,2,1,0:T(8,128)(2,1)S(1)}, bf16[2,4,128,128]{3,2,1,0:T(8,128)(2,1)S(1)}, bf16[2,4,128,128]{3,2,1,0:T(8,128)(2,1)S(1)}, bf16[2,4,128,128]{3,2,1,0:T(8,128)(2,1)S(1)}) custom-call(s32[4]{0:T(128)S(1)} %pad_add_fusion.place_ref, bf16[6,32,1024]{2,1,0:T(8,128)(2,1)S(1)} %constant_dynamic-update-slice_fusion.2.refs_0_, ...), custom_call_target="tpu_custom_call" | custom-call | flops 1000 | bytes 1000 | tf_op jit(solution)/shard_map/data_by_row/pallas_call | solution.py:216
  126.4 1.9 %collective-permute-start.21 = (bf16[2,4,128,128]{3,2,1,0:T(8,128)(2,1)}, bf16[2,4,128,128]{3,2,1,0:T(8,128)(2,1)S(1)}, u32[]{:S(2)}, u32[]{:S(2)}) collective-permute-start(bf16[2,4,128,128]{3,2,1,0:T(8,128)(2,1)} %copy-done.13), channel_id=1, source_target_pairs={{0,32},{16,48},{32,0},{48,16},{1,33},{17,49},{33,1},{49,17},{2,34}... | collective-permute-start | bytes 786440 | tf_op jit(solution)/shard_map/ppermute | solution.py:41
  128.3 2.1 %collective-permute-start.22 = (bf16[2,4,128,128]{3,2,1,0:T(8,128)(2,1)}, bf16[2,4,128,128]{3,2,1,0:T(8,128)(2,1)S(1)}, u32[]{:S(2)}, u32[]{:S(2)}) collective-permute-start(bf16[2,4,128,128]{3,2,1,0:T(8,128)(2,1)} %copy-done.12), channel_id=1, source_target_pairs={{0,48},{16,0},{32,16},{48,32},{1,49},{17,1},{33,17},{49,33},{2,50}... | collective-permute-start | bytes 786440 | tf_op jit(solution)/shard_map/ppermute | solution.py:41
  135.2 4.3 %collective-permute-done.21 = bf16[2,4,128,128]{3,2,1,0:T(8,128)(2,1)S(1)} collective-permute-done((bf16[2,4,128,128]{3,2,1,0:T(8,128)(2,1)}, bf16[2,4,128,128]{3,2,1,0:T(8,128)(2,1)S(1)}, u32[]{:S(2)}, u32[]{:S(2)}) %collective-permute-start.21) | collective-permute-done | bytes 262176 | tf_op jit(solution)/shard_map/ppermute | solution.py:41
  139.5 1.9 %collective-permute-done.22 = bf16[2,4,128,128]{3,2,1,0:T(8,128)(2,1)S(1)} collective-permute-done((bf16[2,4,128,128]{3,2,1,0:T(8,128)(2,1)}, bf16[2,4,128,128]{3,2,1,0:T(8,128)(2,1)S(1)}, u32[]{:S(2)}, u32[]{:S(2)}) %collective-permute-start.22) | collective-permute-done | bytes 262176 | tf_op jit(solution)/shard_map/ppermute | solution.py:41
  141.5 1.8 %collective-permute-start.27 = (bf16[4,128,128]{2,1,0:T(8,128)(2,1)S(1)}, bf16[4,128,128]{2,1,0:T(8,128)(2,1)S(1)}, u32[]{:S(2)}, u32[]{:S(2)}) collective-permute-start(bf16[4,128,128]{2,1,0:T(8,128)(2,1)S(1)} %get-tuple-element.93), channel_id=1, source_target_pairs={{0,64},{64,0},{1,65},{65,1},{2,66},{66,2},{3,67},{67,3},{4,68},{68... | collective-permute-start | bytes 393224 | tf_op jit(solution)/shard_map/ppermute | solution.py:41
  143.4 3.5 %collective-permute-done.27.far_ref = bf16[4,128,128]{2,1,0:T(8,128)(2,1)S(1)} collective-permute-done((bf16[4,128,128]{2,1,0:T(8,128)(2,1)S(1)}, bf16[4,128,128]{2,1,0:T(8,128)(2,1)S(1)}, u32[]{:S(2)}, u32[]{:S(2)}) %collective-permute-start.27) | collective-permute-done | bytes 131104 | tf_op jit(solution)/shard_map/ppermute | solution.py:41
  146.9 2.7 %collective-permute-start.28 = (bf16[2,4,128,128]{3,2,1,0:T(8,128)(2,1)S(1)}, bf16[2,4,128,128]{3,2,1,0:T(8,128)(2,1)S(1)}, u32[]{:S(2)}, u32[]{:S(2)}) collective-permute-start(bf16[2,4,128,128]{3,2,1,0:T(8,128)(2,1)S(1)} %pad_maximum_fusion.6), channel_id=1, source_target_pairs={{0,8},{8,0},{1,9},{9,1},{2,10},{10,2},{3,11},{11,3},{4,12},{12,4},... | collective-permute-start | bytes 786440 | tf_op jit(solution)/shard_map/ppermute | solution.py:41
  152.3 1.9 %place.1 = bf16[4,64,512]{2,1,0:T(8,128)(2,1)} custom-call(s32[4]{0:T(128)S(1)} %pad_add_fusion.place_ref, bf16[512,512]{1,0:T(8,128)(2,1)S(1)} %orders.1.order_ref, bf16[4,128,128]{2,1,0:T(8,128)(2,1)S(1)} %get-tuple-element.92.own_ref, bf16[4,128,128]{2,1,0:T(8,128)(2,1)S(1)} %collective-permute-done.27.far_ref, ...), custom_call_target="tpu_custom_call" | custom-call | flops 1000 | bytes 1000 | tf_op jit(solution)/shard_map/place/pallas_call | solution.py:371
  (114 shorter events, 35.8 us)
Async XLA Ops:
  1.8 14.5 %collective-permute-start.2 = (bf16[4,32,1024]{2,1,0:T(8,128)(2,1)S(1)}, bf16[4,32,1024]{2,1,0:T(8,128)(2,1)S(1)}, u32[]{:S(2)}, u32[]{:S(2)}) collective-permute-start(bf16[4,32,1024]{2,1,0:T(8,128)(2,1)S(1)} %bitcast.61), channel_id=1, source_target_pairs={{0,64},{64,0},{1,65},{65,1},{2,66},{66,2},{3,67},{67,3},{4,68},{68... | collective-permute-start | bytes 786440 | tf_op jit(solution)/shard_map/ppermute | solution.py:41
  5.6 6.4 %collective-permute-start = (bf16[1,32,1024]{2,1,0:T(8,128)(2,1)S(1)}, bf16[1,32,1024]{2,1,0:T(8,128)(2,1)S(1)}, u32[]{:S(2)}, u32[]{:S(2)}) collective-permute-start(bf16[1,32,1024]{2,1,0:T(8,128)(2,1)S(1)} %get-tuple-element.96), channel_id=1, source_target_pairs={{0,1},{1,2},{2,3},{3,4},{4,5},{5,6},{6,7},{8,9},{9,10},{10,11},{11... | collective-permute-start | bytes 196616 | tf_op jit(solution)/shard_map/ppermute | solution.py:311
  7.9 6.7 %collective-permute-start.1 = (bf16[1,32,1024]{2,1,0:T(8,128)(2,1)S(1)}, bf16[1,32,1024]{2,1,0:T(8,128)(2,1)S(1)}, u32[]{:S(2)}, u32[]{:S(2)}) collective-permute-start(bf16[1,32,1024]{2,1,0:T(8,128)(2,1)S(1)} %get-tuple-element.97), channel_id=1, source_target_pairs={{1,0},{2,1},{3,2},{4,3},{5,4},{6,5},{7,6},{9,8},{10,9},{11,10},{12... | collective-permute-start | bytes 196616 | tf_op jit(solution)/shard_map/ppermute | solution.py:312
  14.7 5.4 %collective-permute-start.3 = (bf16[2,32,1024]{2,1,0:T(8,128)(2,1)S(1)}, bf16[2,32,1024]{2,1,0:T(8,128)(2,1)S(1)}, u32[]{:S(2)}, u32[]{:S(2)}) collective-permute-start(bf16[2,32,1024]{2,1,0:T(8,128)(2,1)S(1)} %pad_maximum_fusion.7), channel_id=1, source_target_pairs={{0,64},{64,0},{1,65},{65,1},{2,66},{66,2},{3,67},{67,3},{4,68},{68... | collective-permute-start | bytes 393224 | tf_op jit(solution)/shard_map/ppermute | solution.py:41
  16.2 13.5 %collective-permute-start.5 = (bf16[2,864,128]{2,1,0:T(8,128)(2,1)S(1)}, bf16[2,864,128]{2,1,0:T(8,128)(2,1)S(1)}, u32[]{:S(2)}, u32[]{:S(2)}) collective-permute-start(bf16[2,864,128]{2,1,0:T(8,128)(2,1)S(1)} %get-tuple-element.48), channel_id=1, source_target_pairs={{0,64},{64,0},{1,65},{65,1},{2,66},{66,2},{3,67},{67,3},{4,68},{68... | collective-permute-start | bytes 1327112 | tf_op jit(solution)/shard_map/ppermute | solution.py:41
  20.2 17.3 %collective-permute-start.4 = (bf16[2,6,32,1024]{3,2,1,0:T(8,128)(2,1)S(1)}, bf16[2,6,32,1024]{3,2,1,0:T(8,128)(2,1)S(1)}, u32[]{:S(2)}, u32[]{:S(2)}) collective-permute-start(bf16[2,6,32,1024]{3,2,1,0:T(8,128)(2,1)S(1)} %pad_maximum_fusion), channel_id=1, source_target_pairs={{0,8},{8,0},{1,9},{9,1},{2,10},{10,2},{3,11},{11,3},{4,12},{12,4},... | collective-permute-start | bytes 2359304 | tf_op jit(solution)/shard_map/ppermute | solution.py:41
  24.6 23.4 %collective-permute-start.10 = (bf16[8,32,1024]{2,1,0:T(8,128)(2,1)S(1)}, bf16[8,32,1024]{2,1,0:T(8,128)(2,1)S(1)}, u32[]{:S(2)}, u32[]{:S(2)}) collective-permute-start(bf16[8,32,1024]{2,1,0:T(8,128)(2,1)S(1)} %pad_maximum_fusion.2.refs_3_), channel_id=1, source_target_pairs={{0,48},{16,0},{32,16},{48,32},{1,49},{17,1},{33,17},{49,33},{2,50}... | collective-permute-start | bytes 1572872 | tf_op jit(solution)/shard_map/ppermute | solution.py:41
  29.8 7.7 %collective-permute-start.6 = (bf16[2,864,128]{2,1,0:T(8,128)(2,1)S(1)}, bf16[2,864,128]{2,1,0:T(8,128)(2,1)S(1)}, u32[]{:S(2)}, u32[]{:S(2)}) collective-permute-start(bf16[2,864,128]{2,1,0:T(8,128)(2,1)S(1)} %pad_maximum_fusion.3), channel_id=1, source_target_pairs={{0,8},{8,0},{1,9},{9,1},{2,10},{10,2},{3,11},{11,3},{4,12},{12,4},... | collective-permute-start | bytes 1327112 | tf_op jit(solution)/shard_map/ppermute | solution.py:41
  31.9 16.3 %collective-permute-start.11 = (bf16[8,32,1024]{2,1,0:T(8,128)(2,1)S(1)}, bf16[8,32,1024]{2,1,0:T(8,128)(2,1)S(1)}, u32[]{:S(2)}, u32[]{:S(2)}) collective-permute-start(bf16[8,32,1024]{2,1,0:T(8,128)(2,1)S(1)} %pad_maximum_fusion.2.refs_3_), channel_id=1, source_target_pairs={{0,32},{16,48},{32,0},{48,16},{1,33},{17,49},{33,1},{49,17},{2,34}... | collective-permute-start | bytes 1572872 | tf_op jit(solution)/shard_map/ppermute | solution.py:41
  34.7 23.9 %collective-permute-start.12 = (bf16[8,32,1024]{2,1,0:T(8,128)(2,1)S(1)}, bf16[8,32,1024]{2,1,0:T(8,128)(2,1)S(1)}, u32[]{:S(2)}, u32[]{:S(2)}) collective-permute-start(bf16[8,32,1024]{2,1,0:T(8,128)(2,1)S(1)} %pad_maximum_fusion.2.refs_3_), channel_id=1, source_target_pairs={{0,16},{16,32},{32,48},{48,0},{1,17},{17,33},{33,49},{49,1},{2,18}... | collective-permute-start | bytes 1572872 | tf_op jit(solution)/shard_map/ppermute | solution.py:41
  44.4 22.4 %collective-permute-start.7 = (bf16[4,32,1024]{2,1,0:T(8,128)(2,1)S(1)}, bf16[4,32,1024]{2,1,0:T(8,128)(2,1)S(1)}, u32[]{:S(2)}, u32[]{:S(2)}) collective-permute-start(bf16[4,32,1024]{2,1,0:T(8,128)(2,1)S(1)} %get-tuple-element.56), channel_id=1, source_target_pairs={{0,16},{16,32},{32,48},{48,0},{1,17},{17,33},{33,49},{49,1},{2,18}... | collective-permute-start | bytes 786440 | tf_op jit(solution)/shard_map/ppermute | solution.py:41
  44.4 25.0 %collective-permute-start.8 = (bf16[4,32,1024]{2,1,0:T(8,128)(2,1)S(1)}, bf16[4,32,1024]{2,1,0:T(8,128)(2,1)S(1)}, u32[]{:S(2)}, u32[]{:S(2)}) collective-permute-start(bf16[4,32,1024]{2,1,0:T(8,128)(2,1)S(1)} %get-tuple-element.57), channel_id=1, source_target_pairs={{0,32},{16,48},{32,0},{48,16},{1,33},{17,49},{33,1},{49,17},{2,34}... | collective-permute-start | bytes 786440 | tf_op jit(solution)/shard_map/ppermute | solution.py:41
  48.0 21.5 %collective-permute-start.9 = (bf16[4,32,1024]{2,1,0:T(8,128)(2,1)S(1)}, bf16[4,32,1024]{2,1,0:T(8,128)(2,1)S(1)}, u32[]{:S(2)}, u32[]{:S(2)}) collective-permute-start(bf16[4,32,1024]{2,1,0:T(8,128)(2,1)S(1)} %get-tuple-element.58), channel_id=1, source_target_pairs={{0,48},{16,0},{32,16},{48,32},{1,49},{17,1},{33,17},{49,33},{2,50}... | collective-permute-start | bytes 786440 | tf_op jit(solution)/shard_map/ppermute | solution.py:41
  48.2 21.5 %collective-permute-start.13 = (bf16[2,864,128]{2,1,0:T(8,128)(2,1)S(1)}, bf16[2,864,128]{2,1,0:T(8,128)(2,1)S(1)}, u32[]{:S(2)}, u32[]{:S(2)}) collective-permute-start(bf16[2,864,128]{2,1,0:T(8,128)(2,1)S(1)} %get-tuple-element.65), channel_id=1, source_target_pairs={{0,64},{64,0},{1,65},{65,1},{2,66},{66,2},{3,67},{67,3},{4,68},{68... | collective-permute-start | bytes 1327112 | tf_op jit(solution)/shard_map/ppermute | solution.py:41
  69.7 13.7 %collective-permute-start.16 = (bf16[4,32,1024]{2,1,0:T(8,128)(2,1)S(1)}, bf16[4,32,1024]{2,1,0:T(8,128)(2,1)S(1)}, u32[]{:S(2)}, u32[]{:S(2)}) collective-permute-start(bf16[4,32,1024]{2,1,0:T(8,128)(2,1)S(1)} %select_convert_fusion), channel_id=1, source_target_pairs={{0,64},{64,0},{1,65},{65,1},{2,66},{66,2},{3,67},{67,3},{4,68},{68... | collective-permute-start | bytes 786440 | tf_op jit(solution)/shard_map/ppermute | solution.py:41
  71.4 5.5 %collective-permute-start.14 = (bf16[1,32,1024]{2,1,0:T(8,128)(2,1)S(1)}, bf16[1,32,1024]{2,1,0:T(8,128)(2,1)S(1)}, u32[]{:S(2)}, u32[]{:S(2)}) collective-permute-start(bf16[1,32,1024]{2,1,0:T(8,128)(2,1)S(1)} %get-tuple-element.95), channel_id=1, source_target_pairs={{0,1},{1,2},{2,3},{3,4},{4,5},{5,6},{6,7},{8,9},{9,10},{10,11},{11... | collective-permute-start | bytes 196616 | tf_op jit(solution)/shard_map/ppermute | solution.py:311
  74.3 6.1 %collective-permute-start.15 = (bf16[1,32,1024]{2,1,0:T(8,128)(2,1)S(1)}, bf16[1,32,1024]{2,1,0:T(8,128)(2,1)S(1)}, u32[]{:S(2)}, u32[]{:S(2)}) collective-permute-start(bf16[1,32,1024]{2,1,0:T(8,128)(2,1)S(1)} %get-tuple-element.94), channel_id=1, source_target_pairs={{1,0},{2,1},{3,2},{4,3},{5,4},{6,5},{7,6},{9,8},{10,9},{11,10},{12... | collective-permute-start | bytes 196616 | tf_op jit(solution)/shard_map/ppermute | solution.py:312
  80.5 5.4 %collective-permute-start.17 = (bf16[2,32,1024]{2,1,0:T(8,128)(2,1)S(1)}, bf16[2,32,1024]{2,1,0:T(8,128)(2,1)S(1)}, u32[]{:S(2)}, u32[]{:S(2)}) collective-permute-start(bf16[2,32,1024]{2,1,0:T(8,128)(2,1)S(1)} %pad_maximum_fusion.8), channel_id=1, source_target_pairs={{0,64},{64,0},{1,65},{65,1},{2,66},{66,2},{3,67},{67,3},{4,68},{68... | collective-permute-start | bytes 393224 | tf_op jit(solution)/shard_map/ppermute | solution.py:41
  86.8 11.6 %collective-permute-start.18 = (bf16[2,6,32,1024]{3,2,1,0:T(8,128)(2,1)}, bf16[2,6,32,1024]{3,2,1,0:T(8,128)(2,1)S(1)}, u32[]{:S(2)}, u32[]{:S(2)}) collective-permute-start(bf16[2,6,32,1024]{3,2,1,0:T(8,128)(2,1)} %pad_maximum_fusion.1), channel_id=1, source_target_pairs={{0,8},{8,0},{1,9},{9,1},{2,10},{10,2},{3,11},{11,3},{4,12},{12,4},... | collective-permute-start | bytes 2359304 | tf_op jit(solution)/shard_map/ppermute | solution.py:41
  91.6 22.3 %all-to-all-start = ((bf16[4,2,144,384]{3,2,1,0:T(8,128)(2,1)}), bf16[4,2,144,384]{3,2,1,0:T(8,128)(2,1)}, u32[]{:S(2)}, u32[]{:S(2)}) async-start(bf16[4,2,144,384]{3,2,1,0:T(8,128)(2,1)} %filter_sums.2), calls=%async_computation | async-start | bytes 1769472 | tf_op jit(solution)/shard_map/all_to_all | solution.py:422
  98.1 17.3 %collective-permute-start.19 = (bf16[2,864,128]{2,1,0:T(8,128)(2,1)}, bf16[2,864,128]{2,1,0:T(8,128)(2,1)}, u32[]{:S(2)}, u32[]{:S(2)}) collective-permute-start(bf16[2,864,128]{2,1,0:T(8,128)(2,1)} %pad_maximum_fusion.4), channel_id=1, source_target_pairs={{0,8},{8,0},{1,9},{9,1},{2,10},{10,2},{3,11},{11,3},{4,12},{12,4},... | collective-permute-start | bytes 1327112 | tf_op jit(solution)/shard_map/ppermute | solution.py:41
  108.6 15.4 %collective-permute-start.23 = (bf16[2,144,384]{2,1,0:T(8,128)(2,1)}, bf16[2,144,384]{2,1,0:T(8,128)(2,1)}, u32[]{:S(2)}, u32[]{:S(2)}) collective-permute-start(bf16[2,144,384]{2,1,0:T(8,128)(2,1)} %get-tuple-element.68), channel_id=1, source_target_pairs={{0,2},{2,4},{4,6},{6,0},{1,3},{3,5},{5,7},{7,1},{8,10},{10,12},{12... | collective-permute-start | bytes 663560 | tf_op jit(solution)/shard_map/ppermute | solution.py:41
  110.4 13.7 %collective-permute-start.24 = (bf16[2,144,384]{2,1,0:T(8,128)(2,1)}, bf16[2,144,384]{2,1,0:T(8,128)(2,1)}, u32[]{:S(2)}, u32[]{:S(2)}) collective-permute-start(bf16[2,144,384]{2,1,0:T(8,128)(2,1)} %get-tuple-element.69), channel_id=1, source_target_pairs={{0,4},{2,6},{4,0},{6,2},{1,5},{3,7},{5,1},{7,3},{8,12},{10,14},{12... | collective-permute-start | bytes 663560 | tf_op jit(solution)/shard_map/ppermute | solution.py:41
  112.8 11.3 %collective-permute-start.25 = (bf16[2,144,384]{2,1,0:T(8,128)(2,1)}, bf16[2,144,384]{2,1,0:T(8,128)(2,1)}, u32[]{:S(2)}, u32[]{:S(2)}) collective-permute-start(bf16[2,144,384]{2,1,0:T(8,128)(2,1)} %get-tuple-element.70), channel_id=1, source_target_pairs={{0,6},{2,0},{4,2},{6,4},{1,7},{3,1},{5,3},{7,5},{8,14},{10,8},{12,... | collective-permute-start | bytes 663560 | tf_op jit(solution)/shard_map/ppermute | solution.py:41
  125.7 6.2 %collective-permute-start.26 = (bf16[2,144,384]{2,1,0:T(8,128)(2,1)S(1)}, bf16[2,144,384]{2,1,0:T(8,128)(2,1)S(1)}, u32[]{:S(2)}, u32[]{:S(2)}) collective-permute-start(bf16[2,144,384]{2,1,0:T(8,128)(2,1)S(1)} %fusion.4), channel_id=1, source_target_pairs={{0,1},{1,0},{2,3},{3,2},{4,5},{5,4},{6,7},{7,6},{8,9},{9,8},{10,11... | collective-permute-start | bytes 663560 | tf_op jit(solution)/shard_map/ppermute | solution.py:41
  126.4 8.8 %collective-permute-start.20 = (bf16[2,4,128,128]{3,2,1,0:T(8,128)(2,1)}, bf16[2,4,128,128]{3,2,1,0:T(8,128)(2,1)S(1)}, u32[]{:S(2)}, u32[]{:S(2)}) collective-permute-start(bf16[2,4,128,128]{3,2,1,0:T(8,128)(2,1)} %copy-done.14), channel_id=1, source_target_pairs={{0,16},{16,32},{32,48},{48,0},{1,17},{17,33},{33,49},{49,1},{2,18}... | collective-permute-start | bytes 786440 | tf_op jit(solution)/shard_map/ppermute | solution.py:41
  126.4 13.1 %collective-permute-start.21 = (bf16[2,4,128,128]{3,2,1,0:T(8,128)(2,1)}, bf16[2,4,128,128]{3,2,1,0:T(8,128)(2,1)S(1)}, u32[]{:S(2)}, u32[]{:S(2)}) collective-permute-start(bf16[2,4,128,128]{3,2,1,0:T(8,128)(2,1)} %copy-done.13), channel_id=1, source_target_pairs={{0,32},{16,48},{32,0},{48,16},{1,33},{17,49},{33,1},{49,17},{2,34}... | collective-permute-start | bytes 786440 | tf_op jit(solution)/shard_map/ppermute | solution.py:41
  128.3 13.0 %collective-permute-start.22 = (bf16[2,4,128,128]{3,2,1,0:T(8,128)(2,1)}, bf16[2,4,128,128]{3,2,1,0:T(8,128)(2,1)S(1)}, u32[]{:S(2)}, u32[]{:S(2)}) collective-permute-start(bf16[2,4,128,128]{3,2,1,0:T(8,128)(2,1)} %copy-done.12), channel_id=1, source_target_pairs={{0,48},{16,0},{32,16},{48,32},{1,49},{17,1},{33,17},{49,33},{2,50}... | collective-permute-start | bytes 786440 | tf_op jit(solution)/shard_map/ppermute | solution.py:41
  133.0 16.6 %collective-permute-start.29 = (bf16[2,2,36,384]{3,2,1,0:T(8,128)(2,1)S(1)}, bf16[2,2,36,384]{3,2,1,0:T(8,128)(2,1)S(1)}, u32[]{:S(2)}, u32[]{:S(2)}) collective-permute-start(bf16[2,2,36,384]{3,2,1,0:T(8,128)(2,1)S(1)} %slice_bitcast_fusion.1), channel_id=1, source_target_pairs={{0,64},{64,0},{1,65},{65,1},{2,66},{66,2},{3,67},{67,3},{4,68},{68... | collective-permute-start | bytes 331784 | tf_op jit(solution)/shard_map/ppermute | solution.py:41
  141.5 5.4 %collective-permute-start.27 = (bf16[4,128,128]{2,1,0:T(8,128)(2,1)S(1)}, bf16[4,128,128]{2,1,0:T(8,128)(2,1)S(1)}, u32[]{:S(2)}, u32[]{:S(2)}) collective-permute-start(bf16[4,128,128]{2,1,0:T(8,128)(2,1)S(1)} %get-tuple-element.93), channel_id=1, source_target_pairs={{0,64},{64,0},{1,65},{65,1},{2,66},{66,2},{3,67},{67,3},{4,68},{68... | collective-permute-start | bytes 393224 | tf_op jit(solution)/shard_map/ppermute | solution.py:41
  146.9 5.4 %collective-permute-start.28 = (bf16[2,4,128,128]{3,2,1,0:T(8,128)(2,1)S(1)}, bf16[2,4,128,128]{3,2,1,0:T(8,128)(2,1)S(1)}, u32[]{:S(2)}, u32[]{:S(2)}) collective-permute-start(bf16[2,4,128,128]{3,2,1,0:T(8,128)(2,1)S(1)} %pad_maximum_fusion.6), channel_id=1, source_target_pairs={{0,8},{8,0},{1,9},{9,1},{2,10},{10,2},{3,11},{11,3},{4,12},{12,4},... | collective-permute-start | bytes 786440 | tf_op jit(solution)/shard_map/ppermute | solution.py:41
  149.7 1.4 collective-permute-start.30
  (19 other events, 91.1 us)
